TPU v7x, 32 devices: a whole 2x2x4 slice. The times are simulated.
32 devices in a mesh: pencil: 8 (over z, y), lev: 4 (over x, core).
Axes of the slice: x: 2, y: 2, z: 4, core: 2. Of those that a mesh axis runs over, the one named last changes fastest.
Arguments:
- background_std: float32 [4, 4096, 2048], P('lev', 'pencil'), may hold values from 0.4 to 6.1
- x_kernel: float32 [4, 31], P('lev'), may hold values from -0.06 to 0.12
- y_kernel: float32 [4, 31], P('lev'), may hold values from -0.06 to 0.12
- obs_owner: int32 [8192, 1], P(('pencil', 'lev')), may hold values from 0 to 7; in each aligned block of 256 rows (0 to 255, 256 to 511, ...) at most 64 rows name the same one
- obs_cells: int32 [8192, 16], P(('pencil', 'lev')), may hold values from 0 to 1048575, as said below
- obs_weights: float32 [8192, 16], P(('pencil', 'lev')), may hold values from -0.05 to 0.2
- innovation: float32 [8192], P(('pencil', 'lev')), may hold values from -6 to 6
- obs_precision: float32 [8192], P(('pencil', 'lev')), may hold values from 0.25 to 4
- obs_counts: int32 [32], P(('pencil', 'lev')), may hold values from 129 to 256, as said below
Outputs:
- control: float32 [4, 2048, 4096], P('lev', 'pencil')
- increment: float32 [4, 4096, 2048], P('lev', 'pencil')
Inputs may be any that keep to these rules, and one draw needn't show every extreme that they name: `obs_owner`: no device holds more than 64 observations of one owner, and some device reaches 64. `obs_cells`: indices into the owner's tile of 1 slabs by 512 columns by 2048 rows, flattened in that order. `obs_counts`: some device has all 256 slots live.
All inputs are finite; a program needn't handle non-finite values.
Results may differ from a plain program's by a relative error of at most 0.0001.
Values sent between devices are 32-bit elements; how exact they have to be, the bound alone decides.
No kernel may reach another device: no remote copies, remote signals or barrier semaphores. Data moves between devices by JAX's collectives and lax.ppermute only.
A program may use at most 64 MiB of HBM per device.

v0:
```python
import functools

import jax
import jax.numpy as jnp
import numpy as np
from jax import lax
from jax.experimental import pallas as pl
from jax.experimental.pallas import tpu as pltpu
from jax.sharding import PartitionSpec as P


BF = jnp.bfloat16
F32 = jnp.float32
I32 = jnp.int32
LANES = 128
WIDE = 256
HALO = 32
PAD = 16
PACK = 40
GROUP = 8
COPIES = 4
PAIR = 2
BATCH = 4
CODES = 40
VMEM_LIMIT = 58 * 1024 * 1024


def vmem():
    return pl.BlockSpec(memory_space=pltpu.VMEM)


def smem():
    return pl.BlockSpec(memory_space=pltpu.SMEM)


def hbm():
    return pl.BlockSpec(memory_space=pl.ANY)


def params():
    return pltpu.CompilerParams(vmem_limit_bytes=VMEM_LIMIT)


def split2(x):
    high = x.astype(BF)
    return high, (x - high.astype(F32)).astype(BF)


def split3(x):
    high = x.astype(BF)
    rest = x - high.astype(F32)
    mid = rest.astype(BF)
    return high, mid, (rest - mid.astype(F32)).astype(BF)


def mm(a, b):
    return jnp.dot(a, b, preferred_element_type=F32)


def mm_parts(a_parts, b_parts):
    (ah, al), (bh, bl) = a_parts, b_parts
    return mm(ah, bh) + (mm(al, bh) + mm(ah, bl))


def iota(shape, dim):
    return lax.broadcasted_iota(I32, shape, dim)


def pack_kernel(
    counts, owner, cells, weights, depart, prec, out, *, parts, columns, height, margin
):
    stencil, hold = cells.shape
    shift = height.bit_length() - 1
    block = height // parts
    reach = 2 * margin
    row_id = iota((hold, hold), 0)
    col_id = iota((hold, hold), 1)
    eye = row_id == col_id
    col_f = col_id.astype(F32)
    live = iota((1, hold), 1) < counts[0]
    cell = cells[...]
    column = lax.shift_right_logical(cell, jnp.full(cell.shape, shift, I32))
    row = cell & (height - 1)

    def any_of(mask):
        return jnp.max(jnp.where(mask, 1.0, 0.0), axis=0, keepdims=True)

    def turn(line):
        return jnp.sum(jnp.where(eye, line, 0.0), axis=1, keepdims=True)

    left = any_of(column < reach)
    right = any_of(column >= columns - reach)
    side = left + 3.0 * right - 2.0 * left * right
    base = jnp.where(live, owner[...].astype(F32) * 4.0, 4.0 * parts)
    key = jnp.where(live, base + side, base)
    key_col = turn(key)
    before = (key_col < key) | ((key_col == key) & (row_id < col_id))
    rank = jnp.sum(jnp.where(before, 1.0, 0.0), axis=0, keepdims=True)
    begin = jnp.sum(jnp.where(key_col < base, 1.0, 0.0), axis=0, keepdims=True)
    rank_col = turn(rank)
    perm = jnp.where(rank_col == col_f, 1.0, 0.0).astype(BF)

    def sort(values):
        total = None
        for part in split3(values):
            term = mm(part, perm)
            total = term if total is None else total + term
        return total

    weight = jnp.where(live, prec[...], 0.0)
    rest = [weight * depart[...], weight, key, rank - begin, jnp.zeros((4, hold), F32)]
    values = [cell.astype(F32), weights[...]] + rest
    ordered = sort(jnp.concatenate(values, axis=0))
    line = iota((8, hold), 0)
    tail = ordered[2 * stencil : 2 * stencil + 8, :]
    first_half = col_f < float(LANES)
    fourfold = 4.0 * jnp.where(first_half, col_f, col_f - float(LANES))
    for i, (low, high) in enumerate(((0.0, 4.0), (1.0, 3.0), (2.0, 2.0))):
        bound = fourfold + jnp.where(first_half, low, high)
        begins = jnp.sum(jnp.where(key_col < bound, 1.0, 0.0), axis=0, keepdims=True)
        tail = jnp.where(line == 5 + i, begins, tail)
    last = (line == 7) & (iota((8, hold), 1) == hold - 1)

    def per_part(part, carry):
        low = part * block - margin
        high = (part + 1) * block + margin
        flag = jnp.where(live, any_of((row >= low) & (row < high)), 0.0)
        place = jnp.sum(jnp.where(col_id < row_id, flag, 0.0), axis=1, keepdims=True)
        chosen = (place == col_f) & (turn(flag) > 0.0)
        listed = jnp.sum(jnp.where(chosen, rank_col, 0.0), axis=0, keepdims=True)
        amount = jnp.sum(flag, axis=1, keepdims=True)
        out[part, 0 : 2 * stencil, :] = ordered[0 : 2 * stencil, :]
        out[part, 2 * stencil : 2 * stencil + 8, :] = jnp.where(
            line == 4, listed, jnp.where(last, amount, tail)
        )
        return carry

    lax.fori_loop(0, parts, per_part, 0)


class Layout:
    def __init__(self, senders, hold, stencil, parts):
        lines = hold // LANES
        self.table = 3 * hold
        sizes = dict(
            addr=stencil * lines, rows=stencil * lines, listed=lines, slot=lines, start=3 * lines
        )
        self.ints = {}
        at = 0
        for name, size in sizes.items():
            self.ints[name] = (at, size)
            at += senders * size
        self.int_rows = at
        self.floats = {}
        at = 0
        for name, size in dict(wgt=stencil * lines, val=lines).items():
            self.floats[name] = (at, size)
            at += senders * size
        self.float_rows = at


def unpack_kernel(
    meta,
    recv,
    ints,
    floats,
    own_lines,
    own,
    own_sum,
    line_sum,
    lane_sum,
    *,
    layout,
    parts,
    columns,
    height,
    capacity,
    stencil,
    group,
):
    senders, _, hold = recv.shape
    lines = hold // LANES
    me = meta[0]
    shift = height.bit_length() - 1
    wide = columns + 2 * HALO
    block = height // parts
    high_rows = block + 2 * PAD
    length = columns * parts
    slots = senders * capacity

    def put(ref, place, sender, value):
        begin, size = place
        count = value.shape[0]
        for i in range(lines):
            part = value[:, i * LANES : (i + 1) * LANES]
            if count % 8 == 0:
                at = pl.multiple_of(begin + sender * size + i * count, 8)
                ref[pl.ds(at, count), :] = part
            else:
                for j in range(count):
                    ref[pl.ds(begin + sender * size + i + j * lines, 1), :] = part[j : j + 1]

    def right(x, by):
        return lax.shift_right_logical(x, jnp.full(x.shape, by, I32))

    def nt(a, b):
        return lax.dot_general(a, b, (((1,), (1,)), ((), ())), preferred_element_type=F32)

    own_sum[...] = jnp.zeros(own_sum.shape, F32)
    line_sum[...] = jnp.zeros(line_sum.shape, F32)
    lane_sum[...] = jnp.zeros(lane_sum.shape, F32)
    place = iota((LANES, hold), 0)
    index = iota((LANES, hold), 1)

    def per_sender(sender, carry):
        cell = recv[sender, 0:stencil, :].astype(I32)
        tail = recv[sender, 2 * stencil : 2 * stencil + 8, :]
        whole = tail.astype(I32)
        key = whole[2:3, :]
        pos = whole[3:4, :]
        owner = right(key, 2)
        offset = owner - me
        offset = jnp.where(offset > parts // 2, offset - parts, offset)
        offset = jnp.where(offset < -(parts // 2), offset + parts, offset)
        column = right(cell, shift)
        row = cell & (height - 1)
        at = offset * columns + column + HALO
        addr = jnp.where(
            (at >= 0) & (at < wide),
            (right(row, 7) * wide + at) * LANES + (row & (LANES - 1)),
            (height // LANES) * wide * LANES,
        )
        at_row = row - (block * me - PAD)
        across = owner * columns + column
        rows = jnp.where(
            (at_row >= 0) & (at_row < high_rows) & (owner < parts),
            (right(across, 7) * high_rows + at_row) * LANES + (across & (LANES - 1)),
            (length // LANES) * high_rows * LANES,
        )
        within = lax.rem(sender, group) * capacity + pos
        owner = jnp.minimum(owner, parts - 1)
        put(ints, layout.ints["addr"], sender, addr)
        put(ints, layout.ints["rows"], sender, rows)
        put(ints, layout.ints["listed"], sender, whole[4:5, :])
        put(ints, layout.ints["slot"], sender, owner * (group * capacity) + within)
        put(ints, layout.ints["start"], sender, whole[5:8, :])
        put(floats, layout.floats["wgt"], sender, recv[sender, stencil : 2 * stencil, :])
        put(floats, layout.floats["val"], sender, tail[0:1, :])

        here = iota((1, LANES), 1) == me
        begin = jnp.sum(jnp.where(here, whole[5:6, :LANES], 0), axis=1, keepdims=True)
        end = jnp.sum(jnp.where(here, whole[5:6, LANES : 2 * LANES], 0), axis=1, keepdims=True)
        first_slot = sender * capacity
        block_of = first_slot // LANES
        within = place - (first_slot - block_of * LANES)
        chosen = (within >= 0) & (index == begin + within) & (index < end)
        select = jnp.where(chosen, 1.0, 0.0).astype(BF)
        at_lane = (addr & (LANES - 1)).astype(F32)
        fields = jnp.concatenate([at_lane, recv[sender, stencil : 2 * stencil + 8, :]], axis=0)
        total = None
        for part in split3(fields):
            term = nt(select, part)
            total = term if total is None else total + term
        own_sum[block_of, :, 0:CODES] += total
        lane_sum[block_of] += nt(at_lane.astype(BF), select)
        total = None
        for part in split2(right(addr, 7).astype(F32)):
            term = nt(part, select)
            total = term if total is None else total + term
        line_sum[block_of] += total
        return carry

    lax.fori_loop(0, senders, per_sender, 0)

    number = iota((stencil, LANES), 0).astype(F32)
    nowhere = float((height // LANES) * wide)
    for i in range(slots // LANES):
        line = line_sum[i]
        leader = jnp.zeros(line.shape, F32)
        for k in reversed(range(stencil)):
            leader = jnp.where(line == line[k : k + 1, :], float(k), leader)
        leads = jnp.where(leader == number, 1.0, 0.0)
        count = jnp.zeros((1, LANES), F32)
        ranks = []
        for k in range(stencil):
            ranks.append(count)
            count = count + leads[k : k + 1, :]
        place = jnp.zeros(line.shape, F32)
        for k in range(stencil):
            place = jnp.where(leader == float(k), ranks[k], place)
        lists = []
        for k in range(stencil):
            found = jnp.where((leads > 0.0) & (place == float(k)), line, 0.0)
            found = jnp.sum(found, axis=0, keepdims=True)
            lists.append(jnp.where(count > float(k), found, nowhere))
        batches = lax.shift_right_logical(
            count.astype(I32) + (BATCH - 1), jnp.full(count.shape, BATCH.bit_length() - 1, I32)
        )
        lists = jnp.concatenate(lists, axis=0).astype(I32)
        top = i * (stencil + 8)
        own_lines[top : top + stencil, :] = lists
        own_lines[top + stencil : top + stencil + 8, :] = jnp.broadcast_to(batches, (8, LANES))
        codes = jnp.concatenate(
            [
                jnp.zeros((CODES, LANES), F32),
                place * float(LANES) + lane_sum[i],
                jnp.zeros((LANES - CODES - stencil, LANES), F32),
            ],
            axis=0,
        )
        own[i * LANES : (i + 1) * LANES, :] = own_sum[i] + codes.T


def band(shape, taps, shift):
    distance = iota(shape, 1) - iota(shape, 0) + shift
    result = jnp.zeros(shape, F32)
    for tap in range(taps.shape[0]):
        result = jnp.where(distance == tap, taps[tap], result)
    return result


def band_rev(shape, taps, shift):
    distance = iota(shape, 0) - iota(shape, 1) + shift
    result = jnp.zeros(shape, F32)
    for tap in range(taps.shape[0]):
        result = jnp.where(distance == tap, taps[tap], result)
    return result


def exact_nt(a, b):
    return lax.dot_general(
        a,
        b,
        (((1,), (1,)), ((), ())),
        precision=lax.Precision.HIGHEST,
        preferred_element_type=F32,
    )


def store_split(ref, index, value):
    high, low = split2(value)
    ref[(0,) + index] = high
    ref[(1,) + index] = low


def bands_kernel(kx, ky, lat2, lon2, lat1, lon1, *, rows_block):
    margin = kx.shape[0] // 2
    window = lat2.shape[2]
    first = band((window, window), ky, margin)
    reach = first[LANES : LANES + WIDE, :]
    place = iota((window, window), 1)
    for variant in range(3):
        kept = first
        if variant == 0:
            kept = jnp.where(place >= LANES, first, 0.0)
        if variant == 2:
            kept = jnp.where(place < LANES + WIDE, first, 0.0)
        store_split(lat2, (variant,), exact_nt(kept, reach))
    size = lon2.shape[1]
    wide = size + 2 * HALO
    depth = (wide + 32 + LANES - 1) // LANES * LANES
    second = band((wide, depth), kx, -(16 - margin))
    store_split(lon2, (), exact_nt(second[HALO : HALO + size, :], second))
    store_split(lat1, (), band_rev((rows_block, rows_block + 2 * PAD), ky, PAD + margin))
    store_split(lon1, (), band((2 * WIDE, WIDE), kx, LANES + margin))


def pairs(low, high, action):
    def step(i, carry):
        one = low + 2 * i
        action(one, jnp.minimum(one + 1, high - 1), one + 1 < high)
        return carry

    lax.fori_loop(0, lax.shift_right_logical(high - low + 1, 1), step, 0)


def zero_all(refs):
    rows = refs[0].shape[0]
    step = 256

    def clear(i, carry):
        for ref in refs:
            ref[pl.ds(pl.multiple_of(i * step, 8), step), :] = jnp.zeros((step, LANES), F32)
        return carry

    whole = rows // step
    lax.fori_loop(0, whole, clear, 0)
    if rows % step:
        for ref in refs:
            ref[whole * step : rows, :] = jnp.zeros((rows % step, LANES), F32)


def scatter_entries(copies, entries, lane):
    for start in range(0, len(entries), len(copies)):
        group = []
        for ref, (address, value) in zip(copies, entries[start : start + len(copies)]):
            line = lax.shift_right_logical(address, 7)
            spread = jnp.where(lane == (address & (LANES - 1)), value, 0.0)
            group.append((ref, line, ref[pl.ds(line, 1), :] + spread))
        for ref, line, value in group:
            ref[pl.ds(line, 1), :] = value


def spot(sender, idx, per, stencil):
    return sender * per + idx + lax.shift_right_logical(idx, 7) * ((stencil - 1) * LANES)


def copy_parts(layout, source, target, place, chunk, chunks, group, sem):
    begin, size = place
    words = group * size * LANES
    at = begin * LANES + chunk * words
    return pltpu.make_async_copy(source.at[pl.ds(at, words)], target, sem)


def apply_kernel(
    *refs, first, layout, columns, height, hold, stencil, capacity, senders, parts, levels
):
    refs = list(refs)

    def take(count):
        taken = refs[:count]
        del refs[:count]
        return taken

    meta, ints, floats, own_lines, own = take(5)
    if not first:
        replies_h, replies = take(2)
    std_h, std_l_h, std_r_h, lat2_h, lon2_h = take(5)
    if not first:
        merged_h = take(1)[0]
    field_h, send = take(2)
    if first:
        info_out, merged_h = take(2)
    addr, wgt, start, lines_s, val = take(5)
    if first:
        std_flat, picked, spread = take(3)
    scale, merged, sums, high_s, low_s, std, std_l, std_r, lat2, lon2, field = take(11)
    copies = take(PAIR)
    sems, in_sems, out_sems, val_sem = take(4)

    me = meta[0]
    wide = columns + 2 * HALO
    blocks = height // LANES
    group = min(GROUP, senders)
    chunks = senders // group
    slots = senders * capacity
    lane = iota((1, LANES), 1)
    per = stencil * hold
    table = layout.table

    def chunk_copies(chunk):
        todo = [
            (ints, addr, layout.ints["addr"]),
            (floats, wgt, layout.floats["wgt"]),
            (ints, start, layout.ints["start"]),
        ]
        if first:
            todo.append((floats, val, layout.floats["val"]))
        return [
            copy_parts(layout, source, target, place, chunk, chunks, group, sems.at[i])
            for i, (source, target, place) in enumerate(todo)
        ]

    def load_chunk(chunk):
        for copy in chunk_copies(chunk):
            copy.start()
        for copy in chunk_copies(chunk):
            copy.wait()

    pending = []
    if chunks == 1:
        pending = chunk_copies(0)
        for copy in pending:
            copy.start()
    operands = [
        pltpu.make_async_copy(source, target, in_sems.at[i])
        for i, (source, target) in enumerate(
            (
                (std_h, std),
                (std_l_h, std_l),
                (std_r_h, std_r),
                (lat2_h, lat2),
                (lon2_h, lon2),
            )
        )
    ]
    own_copy = pltpu.make_async_copy(own_lines, lines_s, in_sems.at[5])
    own_copy.start()
    for copy in operands:
        copy.start()

    def value_copy(owner):
        at = pl.multiple_of(owner * (replies.shape[1] * LANES), 1024)
        return pltpu.make_async_copy(
            replies_h.at[pl.ds(at, slots)], val.at[pl.ds(owner * slots, slots)], val_sem.at[owner]
        )

    def each_owner(action):
        def step(owner, carry):
            action(value_copy(owner))
            return carry

        lax.fori_loop(0, parts, step, 0)

    if not first:
        each_owner(lambda copy: copy.start())
    zero_all(copies)
    zero_all([sums])

    merged_copy = pltpu.make_async_copy(
        *((merged, merged_h) if first else (merged_h, merged)), in_sems.at[6]
    )
    if not first:
        merged_copy.start()

    lane_of = iota((slots, LANES), 1)
    known = own[...]
    column = 2 * stencil if first else 2 * stencil + 2
    scale[...] = jnp.broadcast_to(known[:, column : column + 1], (slots, LANES))
    if first:
        lane_f = iota((8, LANES), 1).astype(F32)

        def build(i, carry):
            top = pl.multiple_of(i * 8, 8)
            info = own[pl.ds(top, 8), :]

            def wide_of(at):
                return jnp.broadcast_to(info[:, at : at + 1], (8, LANES))

            rows = [None] * stencil
            for k in range(stencil):
                weight = wide_of(stencil + k)
                code = wide_of(CODES + k)
                spread[pl.ds(k * slots + top, 8), :] = jnp.where(
                    lane_f == wide_of(k), weight, 0.0
                )
                for place in range(k + 1):
                    term = jnp.where(lane_f + float(LANES * place) == code, weight, 0.0)
                    rows[place] = term if rows[place] is None else rows[place] + term
            for place in range(stencil):
                merged[pl.ds(place * slots + top, 8), :] = rows[place]
            return carry

        lax.fori_loop(0, slots // 8, build, 0)
        merged_copy.start()
    own_copy.wait()
    if not first:
        merged_copy.wait()

    after = lax.rem(me + 1, parts)
    ahead = lax.rem(me + parts - 1, parts)

    def start_of(sender, owner, row, half):
        return start[sender * table + row * hold + half * LANES + owner]

    def entries_of(sender, idx, value):
        base = spot(sender, idx, per, stencil)
        return [
            (addr[base + k * LANES], wgt[base + k * LANES] * value) for k in range(stencil)
        ]

    def own_line(slot, k):
        at = lax.shift_right_logical(slot, 7) * ((stencil + 7) * LANES) + slot
        return lines_s[at + k * LANES]

    def batches_of(one, two):
        return jnp.maximum(own_line(one, stencil), own_line(two, stencil))

    def own_pairs(chunk, action):
        def per_sender(sender, carry):
            amount = start_of(sender, me, 0, 1) - start_of(sender, me, 0, 0)
            base = (chunk * group + sender) * capacity
            pairs(base, base + amount, action)
            return carry

        lax.fori_loop(0, group, per_sender, 0)

    def scatter_own(chunk):
        def action(one, two, has_two):
            second = jnp.where(has_two, 1.0, 0.0)
            values = (scale[pl.ds(one, 1), :], scale[pl.ds(two, 1), :] * second)

            def batch(begin):
                todo = []
                for slot, value, ref in zip((one, two), values, copies):
                    for j in range(BATCH):
                        line = own_line(slot, begin + j)
                        row = merged[pl.ds((begin + j) * slots + slot, 1), :] * value
                        todo.append((ref, line, ref[pl.ds(line, 1), :] + row))
                for ref, line, row in todo:
                    ref[pl.ds(line, 1), :] = row

            def more(i, carry):
                batch(i * BATCH)
                return carry

            batch(0)
            lax.fori_loop(1, batches_of(one, two), more, 0)

        own_pairs(chunk, action)

    def scatter_halo(chunk):
        def per_sender(sender, carry):
            for owner, low, high in ((after, (1, 0), (1, 1)), (ahead, (2, 0), (0, 1))):
                begin = start_of(sender, owner, 0, 0)

                def value_of(idx, owner=owner, begin=begin):
                    if first:
                        return val[sender * hold + idx]
                    place = (chunk * group + sender) * capacity + idx - begin
                    return val[owner * slots + place]

                def action(one, two, has_two, value_of=value_of):
                    second = jnp.where(has_two, value_of(two), 0.0)
                    scatter_entries(
                        copies,
                        entries_of(sender, one, value_of(one)) + entries_of(sender, two, second),
                        lane,
                    )

                pairs(start_of(sender, owner, *low), start_of(sender, owner, *high), action)
            return carry

        lax.fori_loop(0, group, per_sender, 0)

    def scatter_chunk(chunk):
        scatter_own(chunk)
        scatter_halo(chunk)

    def over_chunks(work):
        if chunks == 1:
            work(0)
        else:

            def step(chunk, carry):
                load_chunk(chunk)
                work(chunk)
                return carry

            lax.fori_loop(0, chunks, step, 0)

    for copy in pending:
        copy.wait()
    if not first:
        each_owner(lambda copy: copy.wait())
    over_chunks(scatter_chunk)
    for copy in operands:
        copy.wait()

    for jb in range(blocks):
        lanes = slice(jb * LANES, (jb + 1) * LANES)
        for low, size, source in (
            (0, HALO, std_l),
            (HALO, columns, std),
            (HALO + columns, HALO, std_r),
        ):
            rows = slice(jb * wide + low, jb * wide + low + size)
            total = copies[0][rows, :]
            for ref in copies[1:]:
                total = total + ref[rows, :]
            high, lo = split2(total * source[:, lanes])
            high_s[low : low + size, lanes] = high
            low_s[low : low + size, lanes] = lo
        if first:
            std_flat[jb * wide + HALO : jb * wide + HALO + columns, :] = std[:, lanes]

    smoothed = copies[0]
    size = lon2.shape[1]
    count = height // WIDE
    outgoing = [merged_copy] if first else []
    for block in range(count):
        variant = 0 if block == 0 else (2 if block == count - 1 else 1)
        low = max(block * WIDE - LANES, 0)
        high = min(block * WIDE + WIDE + LANES, height)
        inner = slice(low - (block * WIDE - LANES), high - (block * WIDE - LANES))
        matrix = (lat2[0, variant, inner, :], lat2[1, variant, inner, :])
        along = mm_parts((high_s[:, low:high], low_s[:, low:high]), matrix)
        parts_y = split2(along)
        lanes = slice(block * WIDE, (block + 1) * WIDE)
        for begin in range(0, columns, size):
            some = min(size, columns - begin)
            rows = slice(begin, begin + some)
            window = slice(begin, begin + some + 2 * HALO)
            matrix = tuple(lon2[i, 0:some, 0 : some + 2 * HALO] for i in range(2))
            result = mm_parts(matrix, (parts_y[0][window, :], parts_y[1][window, :]))
            field[rows, lanes] = result
            scaled = result * std[rows, lanes]
            for half in range(WIDE // LANES):
                top = (block * (WIDE // LANES) + half) * wide + HALO + begin
                smoothed[top : top + some, :] = scaled[:, half * LANES : (half + 1) * LANES]
        outgoing.append(
            pltpu.make_async_copy(field.at[:, lanes], field_h.at[:, lanes], out_sems.at[block])
        )
        outgoing[-1].start()

    def gather_chunk(chunk):
        def action(one, two, has_two):
            def batch(begin, totals):
                result = []
                for slot, total in zip((one, two), totals):
                    terms = []
                    for j in range(BATCH):
                        line = own_line(slot, begin + j)
                        row = merged[pl.ds((begin + j) * slots + slot, 1), :]
                        terms.append(row * smoothed[pl.ds(line, 1), :])
                    result.append(total + ((terms[0] + terms[1]) + (terms[2] + terms[3])))
                return tuple(result)

            zero = jnp.zeros((1, LANES), F32)
            totals = lax.fori_loop(
                1,
                batches_of(one, two),
                lambda i, totals: batch(i * BATCH, totals),
                batch(0, (zero, zero)),
            )
            for slot, total in zip((one, two), totals):
                sums[pl.ds(slot, 1), :] = total

        own_pairs(chunk, action)

        if first:

            def per_sender(sender, carry):
                begin = start_of(sender, me, 0, 0)
                amount = start_of(sender, me, 0, 1) - begin
                base = (chunk * group + sender) * capacity

                def pick(idx):
                    slot = base + idx - begin
                    at = spot(sender, idx, per, stencil)
                    for k in range(stencil):
                        line = lax.shift_right_logical(addr[at + k * LANES], 7)
                        row = spread[pl.ds(k * slots + slot, 1), :]
                        picked[pl.ds(k * slots + slot, 1), :] = row * std_flat[pl.ds(line, 1), :]

                def both(one, two, has_two):
                    pick(one)
                    pick(two)

                pairs(begin, begin + amount, both)
                return carry

            lax.fori_loop(0, group, per_sender, 0)

    over_chunks(gather_chunk)

    def whole(x):
        return jnp.sum(x, axis=0, keepdims=True)

    total = jnp.sum(sums[...], axis=1, keepdims=True)
    lines = slots // LANES
    known = own[...]
    source, weight, reply, image0 = (
        known[:, 2 * stencil + i : 2 * stencil + i + 1] for i in range(4)
    )
    if first:
        reply = weight * total
        known = jnp.where(lane_of == 2 * stencil + 2, reply, known)
        known = jnp.where(lane_of == 2 * stencil + 3, total, known)
        info_out[...] = known
        turned = known.T[2 * stencil + 2 : 2 * stencil + 3, :]
        message = [turned[:, i * LANES : (i + 1) * LANES] for i in range(lines)]
        message.append(
            jnp.where(
                lane == 0, whole(source * total), jnp.where(lane == 1, whole(reply * total), 0.0)
            )
        )
        message.append(jnp.zeros((8 - len(message), LANES), F32))
        ones = jnp.ones((8, LANES), BF)
        for k in range(stencil):
            row = None
            for part in split3(picked[k * slots : (k + 1) * slots, :]):
                term = lax.dot_general(
                    ones, part, (((1,), (1,)), ((), ())), preferred_element_type=F32
                )
                row = term if row is None else row + term
            for i in range(lines):
                message.append(row[0:1, i * LANES : (i + 1) * LANES])
        message = jnp.concatenate(message, axis=0)
    else:
        slab = jnp.sum(replies[:, 0:8, :], axis=0)[lines : lines + 1, :]
        length = slab[:, 0:1] / (slab[:, 0:1] + slab[:, 1:2])
        both = source + reply
        s_both = image0 + total
        resid = source - length * both
        s_resid = image0 - length * s_both
        values = [
            resid * s_resid,
            resid * s_both,
            both * s_both,
            resid * image0,
            both * image0,
            weight * s_resid * s_resid,
            weight * s_resid * s_both,
            weight * s_both * s_both,
            weight * s_resid * image0,
            weight * s_both * image0,
            source * image0,
            reply * image0,
        ]
        message = jnp.where(lane == len(values), length, 0.0)
        for i, value in enumerate(values):
            message = jnp.where(lane == i, whole(value), message)
        message = jnp.concatenate([message, jnp.zeros((7, LANES), F32)], axis=0)

    def send_to(i, carry):
        send[i] = message
        return carry

    lax.fori_loop(0, send.shape[0], send_to, 0)
    for copy in outgoing:
        copy.wait()


def final_kernel(
    ints,
    floats,
    replies_h,
    totals,
    std_h,
    field0_h,
    field1_h,
    lat1,
    lon1,
    control_h,
    increment_h,
    addr,
    listed,
    start,
    slot,
    val,
    factors,
    std,
    field0,
    field1,
    control,
    high_s,
    low_s,
    *rest,
    layout,
    hold,
    stencil,
    capacity,
    senders,
    parts,
    length,
):
    copies = rest[:COPIES]
    sems, in_sems, out_sems = rest[COPIES:]
    group = min(GROUP, senders)
    chunks = senders // group
    per = stencil * hold
    rows_block = control.shape[0]
    high_rows = rows_block + 2 * PAD
    lane = iota((1, LANES), 1)
    stride = group * capacity
    owner_words = factors.shape[0] // parts
    to_factors = owner_words - stencil * stride

    def chunk_copies(chunk):
        todo = [
            (ints, addr, layout.ints["rows"]),
            (ints, listed, layout.ints["listed"]),
            (ints, start, layout.ints["start"]),
            (ints, slot, layout.ints["slot"]),
            (floats, val, layout.floats["val"]),
        ]
        result = [
            copy_parts(layout, source, target, place, chunk, chunks, group, sems.at[i])
            for i, (source, target, place) in enumerate(todo)
        ]
        words = parts * owner_words
        result.append(
            pltpu.make_async_copy(
                replies_h.at[pl.ds(chunk * words, words)], factors, sems.at[len(todo)]
            )
        )
        return result

    pending = []
    if chunks == 1:
        pending = chunk_copies(0)
        for copy in pending:
            copy.start()
    operands = [
        pltpu.make_async_copy(source, target, in_sems.at[i])
        for i, (source, target) in enumerate(
            ((std_h, std), (field0_h, field0), (field1_h, field1))
        )
    ]
    for copy in operands:
        copy.start()

    slabs = totals.shape[1]
    every = jnp.sum(totals[...], axis=0)
    norm0 = quad0 = None
    for i in range(slabs):
        line = every[i, 0:1, :]
        a, b = line[:, 10:11], line[:, 11:12]
        norm0 = a if norm0 is None else norm0 + a
        quad0 = b if quad0 is None else quad0 + b
    step0 = norm0 / (norm0 + quad0)
    norm1 = cross = quad1 = quad01 = jnp.zeros((1, 1), F32)
    for i in range(slabs):
        line = every[i, 0:1, :]
        v = [line[:, j : j + 1] for j in range(10)]
        shift = totals[0, i, 0:1, 12:13] - step0
        norm1 = norm1 + (v[0] + shift * (2.0 * v[1] + shift * v[2]))
        cross = cross + (v[3] + shift * v[4])
        quad1 = quad1 + (v[5] + shift * (2.0 * v[6] + shift * v[7]))
        quad01 = quad01 + (v[8] + shift * v[9])
    ratio = norm1 / norm0
    curvature = norm1 + quad1 + ratio * (
        2.0 * (cross + quad01) + ratio * (norm0 + quad0)
    )
    step1 = norm1 / curvature
    first = step0 + step1 * (1.0 - step0 + ratio)
    second = -step0 * step1
    first_line = jnp.broadcast_to(first, (1, LANES))
    second_line = jnp.broadcast_to(second, (1, LANES))

    zero_all(copies)

    def scatter_chunk():
        def per_sender(sender, carry):
            def entries_of(at, scale):
                idx = listed[sender * hold + at]
                place = slot[sender * hold + idx]
                place = place + lax.div(place, stride) * (owner_words - stride)
                base = spot(sender, idx, per, stencil)
                z0 = val[sender * hold + idx] * scale
                u = factors[place] * scale
                value = first_line * z0 + second_line * u
                return [
                    (addr[base + k * LANES], factors[place + to_factors + k * stride] * value)
                    for k in range(stencil)
                ]

            def action(one, two, has_two):
                scale = jnp.where(has_two, 1.0, 0.0)
                scatter_entries(copies, entries_of(one, 1.0) + entries_of(two, scale), lane)

            pairs(0, start[sender * layout.table + layout.table - 1], action)
            return carry

        lax.fori_loop(0, group, per_sender, 0)

    if chunks == 1:
        for copy in pending:
            copy.wait()
        scatter_chunk()
    else:

        def step(chunk, carry):
            for copy in chunk_copies(chunk):
                copy.start()
            for copy in chunk_copies(chunk):
                copy.wait()
            scatter_chunk()
            return carry

        lax.fori_loop(0, chunks, step, 0)

    for copy in operands:
        copy.wait()
    increment = field0
    increment[...] = std[...] * (first * field0[...] + second * field1[...])
    outgoing = [pltpu.make_async_copy(increment, increment_h, out_sems.at[0])]
    outgoing[0].start()

    pair = WIDE // LANES
    count = length // WIDE
    for block in range(count):
        pieces = []
        for half in range(pair):
            rows = slice((block * pair + half) * high_rows, (block * pair + half + 1) * high_rows)
            total = copies[0][rows, :]
            for ref in copies[1:]:
                total = total + ref[rows, :]
            pieces.append(total)
        whole = split2(jnp.concatenate(pieces, axis=1))
        size = lat1.shape[1]
        for top in range(0, rows_block, size):
            window = slice(top, top + size + 2 * PAD)
            along = mm_parts((lat1[0], lat1[1]), (whole[0][window, :], whole[1][window, :]))
            high, low = split2(along)
            high_s[top : top + size, block * WIDE : (block + 1) * WIDE] = high
            low_s[top : top + size, block * WIDE : (block + 1) * WIDE] = low

    def window(ref, block):
        low, high = block * WIDE - LANES, (block + 1) * WIDE + LANES
        if low < 0:
            return jnp.concatenate([ref[:, length + low : length], ref[:, 0:high]], axis=1)
        if high > length:
            return jnp.concatenate([ref[:, low:length], ref[:, 0 : high - length]], axis=1)
        return ref[:, low:high]

    every_lanes = 4
    for block in range(count):
        control[:, block * WIDE : (block + 1) * WIDE] = mm_parts(
            (window(high_s, block), window(low_s, block)), (lon1[0], lon1[1])
        )
        if block % every_lanes == every_lanes - 1:
            lanes = slice((block + 1 - every_lanes) * WIDE, (block + 1) * WIDE)
            outgoing.append(
                pltpu.make_async_copy(
                    control.at[:, lanes], control_h.at[:, lanes], out_sems.at[len(outgoing)]
                )
            )
            outgoing[-1].start()
    for copy in outgoing:
        copy.wait()


def body(
    background_std,
    x_kernel,
    y_kernel,
    obs_owner,
    obs_cells,
    obs_weights,
    innovation,
    obs_precision,
    obs_counts,
):
    parts = lax.axis_size("pencil")
    levels = lax.axis_size("lev")
    me = lax.axis_index("pencil")
    _, columns, height = background_std.shape
    hold, stencil = obs_cells.shape
    margin = x_kernel.shape[1] // 2
    capacity = 2 * hold // parts
    senders = parts
    slots = senders * capacity
    rows_block = height // parts
    length = columns * parts
    blocks = height // LANES
    wide = columns + 2 * HALO
    group = min(GROUP, senders)
    chunks = senders // group
    layout = Layout(senders, hold, stencil, parts)
    std = background_std[0]

    packed = pl.pallas_call(
        functools.partial(
            pack_kernel, parts=parts, columns=columns, height=height, margin=margin
        ),
        out_shape=jax.ShapeDtypeStruct((parts, PACK, hold), F32),
        in_specs=[smem()] + [vmem()] * 5,
        out_specs=vmem(),
        compiler_params=params(),
        name="pack",
    )(
        obs_counts,
        obs_owner.T,
        obs_cells.T,
        obs_weights.T,
        innovation[None, :],
        obs_precision[None, :],
    )
    recv = lax.all_to_all(packed, "pencil", split_axis=0, concat_axis=0, tiled=True)

    right = [(p, (p + 1) % parts) for p in range(parts)]
    left = [(p, (p - 1) % parts) for p in range(parts)]
    std_l = lax.ppermute(std[columns - HALO :, :], "pencil", right)
    std_r = lax.ppermute(std[:HALO, :], "pencil", left)

    size = min(columns, WIDE - 2 * HALO)
    row_size = min(rows_block, LANES)
    lat2, lon2, lat1, lon1 = pl.pallas_call(
        functools.partial(bands_kernel, rows_block=row_size),
        out_shape=[
            jax.ShapeDtypeStruct((2, 3, 2 * WIDE, WIDE), BF),
            jax.ShapeDtypeStruct((2, size, size + 2 * HALO), BF),
            jax.ShapeDtypeStruct((2, row_size, row_size + 2 * PAD), BF),
            jax.ShapeDtypeStruct((2, 2 * WIDE, WIDE), BF),
        ],
        in_specs=[smem(), smem()],
        out_specs=[vmem()] * 4,
        compiler_params=params(),
        name="bands",
    )(x_kernel[0], y_kernel[0])

    meta = jnp.reshape(me, (1,)).astype(I32)
    ints, floats, own_lines, own = pl.pallas_call(
        functools.partial(
            unpack_kernel,
            layout=layout,
            parts=parts,
            columns=columns,
            height=height,
            capacity=capacity,
            stencil=stencil,
            group=group,
        ),
        out_shape=[
            jax.ShapeDtypeStruct((layout.int_rows, LANES), I32),
            jax.ShapeDtypeStruct((layout.float_rows, LANES), F32),
            jax.ShapeDtypeStruct((slots // LANES * (stencil + 8), LANES), I32),
            jax.ShapeDtypeStruct((slots, LANES), F32),
        ],
        in_specs=[smem(), vmem()],
        out_specs=[vmem()] * 4,
        scratch_shapes=[
            pltpu.VMEM((slots // LANES, LANES, LANES), F32),
            pltpu.VMEM((slots // LANES, stencil, LANES), F32),
            pltpu.VMEM((slots // LANES, stencil, LANES), F32),
        ],
        compiler_params=params(),
        name="unpack",
    )(meta, recv)
    ints = ints.reshape(-1)
    floats = floats.reshape(-1)
    own_lines = own_lines.reshape(-1)

    acc = pltpu.VMEM((blocks * wide + 8, LANES), F32)
    column_slots = pltpu.VMEM((slots, LANES), F32)
    static = dict(
        layout=layout,
        columns=columns,
        height=height,
        hold=hold,
        stencil=stencil,
        capacity=capacity,
        senders=senders,
        parts=parts,
        levels=levels,
    )
    per = group * stencil * hold
    line = group * hold
    index_scratch = [
        pltpu.SMEM((per,), I32),
        pltpu.SMEM((per,), F32),
        pltpu.SMEM((group * layout.table,), I32),
        pltpu.SMEM((slots * (stencil + 8),), I32),
    ]
    work = (
        [column_slots, pltpu.VMEM((stencil * slots, LANES), F32), column_slots]
        + [pltpu.VMEM((wide, height), BF)] * 2
        + [
            pltpu.VMEM((columns, height), F32),
            pltpu.VMEM((HALO, height), F32),
            pltpu.VMEM((HALO, height), F32),
            pltpu.VMEM(lat2.shape, BF),
            pltpu.VMEM(lon2.shape, BF),
            pltpu.VMEM((columns, height), F32),
        ]
        + [acc] * PAIR
        + [
            pltpu.SemaphoreType.DMA((4,)),
            pltpu.SemaphoreType.DMA((7,)),
            pltpu.SemaphoreType.DMA((height // WIDE,)),
            pltpu.SemaphoreType.DMA((parts,)),
        ]
    )
    field_shape = jax.ShapeDtypeStruct((columns, height), F32)
    reply_rows = 8 + stencil * slots // LANES
    field0, message, info, merged = pl.pallas_call(
        functools.partial(apply_kernel, first=True, **static),
        out_shape=[
            field_shape,
            jax.ShapeDtypeStruct((parts, reply_rows, LANES), F32),
            jax.ShapeDtypeStruct((slots, LANES), F32),
            jax.ShapeDtypeStruct((stencil * slots, LANES), F32),
        ],
        in_specs=[smem()] + [hbm()] * 3 + [vmem()] + [hbm()] * 5,
        out_specs=[hbm()] + [vmem()] * 2 + [hbm()],
        scratch_shapes=index_scratch
        + [
            pltpu.SMEM((line,), F32),
            acc,
            pltpu.VMEM((stencil * slots, LANES), F32),
            pltpu.VMEM((stencil * slots, LANES), F32),
        ]
        + work,
        compiler_params=params(),
        name="apply_first",
    )(meta, ints, floats, own_lines, own, std, std_l, std_r, lat2, lon2)

    replies = lax.all_to_all(message, "pencil", split_axis=0, concat_axis=0, tiled=True)
    back = replies.reshape(-1)

    field1, sums = pl.pallas_call(
        functools.partial(apply_kernel, first=False, **static),
        out_shape=[
            field_shape,
            jax.ShapeDtypeStruct((parts * levels, 8, LANES), F32),
        ],
        in_specs=[smem()] + [hbm()] * 3 + [vmem(), hbm(), vmem()] + [hbm()] * 6,
        out_specs=[hbm(), vmem()],
        scratch_shapes=index_scratch + [pltpu.SMEM((parts * slots,), F32)] + work,
        compiler_params=params(),
        name="apply_second",
    )(
        meta,
        ints,
        floats,
        own_lines,
        info,
        back,
        replies,
        std,
        std_l,
        std_r,
        lat2,
        lon2,
        merged,
    )

    totals = lax.all_to_all(sums, ("pencil", "lev"), split_axis=0, concat_axis=0, tiled=True)
    totals = totals.reshape(parts, levels, 8, LANES)

    by_chunk = back
    if chunks > 1:
        by_chunk = jnp.concatenate(
            [replies[:, : slots // LANES, :], replies[:, 8:, :]], axis=1
        ).reshape(parts, stencil + 1, chunks, group * capacity)
        by_chunk = jnp.transpose(by_chunk, (2, 0, 1, 3)).reshape(-1)
    owner_words = by_chunk.shape[0] // (chunks * parts)
    high_rows = rows_block + 2 * PAD
    acc_rows = pltpu.VMEM(((length // LANES) * high_rows + 8, LANES), F32)
    control, increment = pl.pallas_call(
        functools.partial(
            final_kernel,
            layout=layout,
            hold=hold,
            stencil=stencil,
            capacity=capacity,
            senders=senders,
            parts=parts,
            length=length,
        ),
        out_shape=[
            jax.ShapeDtypeStruct((rows_block, length), F32),
            field_shape,
        ],
        in_specs=[hbm()] * 3 + [vmem()] + [hbm()] * 3 + [vmem()] * 2,
        out_specs=[hbm()] * 2,
        scratch_shapes=[
            pltpu.SMEM((per,), I32),
            pltpu.SMEM((line,), I32),
            pltpu.SMEM((group * layout.table,), I32),
            pltpu.SMEM((line,), I32),
            pltpu.SMEM((line,), F32),
            pltpu.SMEM((parts * owner_words,), F32),
            pltpu.VMEM((columns, height), F32),
            pltpu.VMEM((columns, height), F32),
            pltpu.VMEM((columns, height), F32),
            pltpu.VMEM((rows_block, length), F32),
            pltpu.VMEM((rows_block, length), BF),
            pltpu.VMEM((rows_block, length), BF),
        ]
        + [acc_rows] * COPIES
        + [
            pltpu.SemaphoreType.DMA((7,)),
            pltpu.SemaphoreType.DMA((3,)),
            pltpu.SemaphoreType.DMA((1 + length // WIDE,)),
        ],
        compiler_params=params(),
        name="outputs",
    )(ints, floats, by_chunk, totals, std, field0, field1, lat1, lon1)
    return control[None], increment[None]


def solution(mesh):
    return jax.shard_map(
        body,
        mesh=mesh,
        in_specs=(
            P("lev", "pencil", None),
            P("lev", None),
            P("lev", None),
            P(("pencil", "lev"), None),
            P(("pencil", "lev"), None),
            P(("pencil", "lev"), None),
            P(("pencil", "lev")),
            P(("pencil", "lev")),
            P(("pencil", "lev")),
        ),
        out_specs=(P("lev", "pencil", None), P("lev", "pencil", None)),
        check_vma=False,
    )
```

profile of v0, /device:TPU:0, one launch (start us, length us, event | category | flops | bytes accessed | tf_op | source)
XLA Modules:
  0.0 171.4 jit_solution(18087891265582891465)
XLA Ops:
  1.3 3.3 %pack.1 = f32[8,40,256]{2,1,0:T(8,128)} custom-call(s32[1]{0:T(128)S(6)} %copy.11.counts, s32[1,256]{1,0:T(1,128)} %bitcast.36, s32[16,256]{1,0:T(8,128)} %bitcast.34, f32[16,256]{1,0:T(8,128)} %bitcast.35, f32[1,256]{1,0:T(1,128)} %bitcast.37, f32[1,256]{1,0:T(1,128)} %bitcast.38), custom_call_target="tpu_custom_call" | custom-call | tf_op jit(solution)/shard_map/pack/pallas_call | solution.py:1044
  4.5 7.3 %all-to-all-start = ((f32[8,40,256]{2,1,0:T(8,128)}), f32[8,40,256]{2,1,0:T(8,128)S(1)}, u32[]{:S(2)}, u32[]{:S(2)}) async-start(f32[8,40,256]{2,1,0:T(8,128)} %pack.1), calls=%async_computation | async-start | bytes 655360 | tf_op jit(solution)/shard_map/all_to_all | solution.py:1061
  11.8 1.1 slice_bitcast_fusion
  12.9 4.8 %collective-permute-start.1 = (f32[32,2048]{1,0:T(8,128)S(1)}, f32[32,2048]{1,0:T(8,128)S(1)}, u32[]{:S(2)}, u32[]{:S(2)}) collective-permute-start(f32[32,2048]{1,0:T(8,128)S(1)} %get-tuple-element.34), channel_id=1, source_target_pairs={{0,28},{4,0},{8,4},{12,8},{16,12},{20,16},{24,20},{28,24},{1,29},{... | collective-permute-start | bytes 786440 | tf_op jit(solution)/shard_map/ppermute | solution.py:1066
  17.7 0.0 collective-permute-start
  17.7 6.3 %bands.1 = (bf16[2,3,512,256]{3,2,1,0:T(8,128)(2,1)}, bf16[2,192,256]{2,1,0:T(8,128)(2,1)}, bf16[2,128,160]{2,1,0:T(8,128)(2,1)}, bf16[2,512,256]{2,1,0:T(8,128)(2,1)}) custom-call(f32[31]{0:T(128)} %bitcast.41, f32[31]{0:T(128)} %bitcast.42), custom_call_target="tpu_custom_call" | custom-call | tf_op jit(solution)/shard_map/bands/pallas_call | solution.py:1070
  23.9 0.0 all-to-all-done.recv
  23.9 0.0 copy-start
  23.9 0.7 copy-done
  24.7 4.5 %unpack.1 = (s32[592,128]{1,0:T(8,128)}, f32[272,128]{1,0:T(8,128)}, s32[96,128]{1,0:T(8,128)}, f32[512,128]{1,0:T(8,128)}) custom-call(s32[1]{0:T(128)} %bitcast.meta.refs_0_, f32[8,40,256]{2,1,0:T(8,128)} %copy-done), custom_call_target="tpu_custom_call" | custom-call | tf_op jit(solution)/shard_map/unpack/pallas_call | solution.py:1085
  29.1 0.3 collective-permute-done.1.refs_7_.refs_9_
  29.4 0.0 copy-start.1
  29.4 0.0 collective-permute-done.refs_6_.refs_8_
  29.4 0.0 copy-start.2
  29.4 0.7 copy-done.1
  30.1 0.1 copy-done.2
  30.2 38.7 %apply_first.1 = (f32[512,2048]{1,0:T(8,128)}, f32[8,72,128]{2,1,0:T(8,128)}, f32[512,128]{1,0:T(8,128)}, f32[8192,128]{1,0:T(8,128)}) custom-call(s32[1]{0:T(128)} %bitcast.meta.refs_0_, s32[75776]{0:T(1024)} %bitcast.25, f32[34816]{0:T(1024)} %bitcast.28, s32[12288]{0:T(1024)} %bitcast.32, f32[512,128]{1,0:T(8,128)} %get-tuple-element.21.refs_4_, ...), custom_call_target="tpu_custom_call" | custom-call | tf_op jit(solution)/shard_map/apply_first/pallas_call | solution.py:1158
  68.9 28.5 %all_to_all.15.refs_6_ = f32[8,72,128]{2,1,0:T(8,128)} all-to-all(f32[8,72,128]{2,1,0:T(8,128)} %get-tuple-element.24), channel_id=1, replica_groups=mesh['pencil'=8,'lev'=4] {'pencil'}, dimensions={0} | all-to-all | bytes 589824 | tf_op jit(solution)/shard_map/all_to_all | solution.py:1180
  97.4 27.6 %apply_second.1 = (f32[512,2048]{1,0:T(8,128)}, f32[32,8,128]{2,1,0:T(8,128)}) custom-call(s32[1]{0:T(128)} %bitcast.meta.refs_0_, s32[75776]{0:T(1024)} %bitcast.26, f32[34816]{0:T(1024)} %bitcast.29, s32[12288]{0:T(1024)} %bitcast.33, f32[512,128]{1,0:T(8,128)} %get-tuple-element.25.refs_4_, f32[73728]{0:T(1024)} %bitcast.23, ...), custom_call_target="tpu_custom_call" | custom-call | tf_op jit(solution)/shard_map/apply_second/pallas_call | solution.py:1183
  125.0 17.6 %all_to_all.16 = f32[32,8,128]{2,1,0:T(8,128)} all-to-all(f32[32,8,128]{2,1,0:T(8,128)} %get-tuple-element.27), channel_id=1, replica_groups=mesh['pencil'=8,'lev'=4] {'pencil','lev'}, dimensions={0} | all-to-all | bytes 262144 | tf_op jit(solution)/shard_map/all_to_all | solution.py:1210
  142.6 28.6 %outputs.1 = (f32[256,4096]{1,0:T(8,128)}, f32[512,2048]{1,0:T(8,128)}) custom-call(s32[75776]{0:T(1024)} %bitcast.27, f32[34816]{0:T(1024)} %bitcast.30, f32[73728]{0:T(1024)} %bitcast.24, f32[8,4,8,128]{3,2,1,0:T(8,128)} %bitcast.31, f32[512,2048]{1,0:T(8,128)} %bitcast.22, f32[512,2048]{1,0:T(8,128)} %get-tuple-element.28.field0_h, ...), custom_call_target="tpu_custom_call" | custom-call | tf_op jit(solution)/shard_map/outputs/pallas_call | solution.py:1222
Async XLA Ops:
  4.5 19.4 %all-to-all-start = ((f32[8,40,256]{2,1,0:T(8,128)}), f32[8,40,256]{2,1,0:T(8,128)S(1)}, u32[]{:S(2)}, u32[]{:S(2)}) async-start(f32[8,40,256]{2,1,0:T(8,128)} %pack.1), calls=%async_computation | async-start | bytes 655360 | tf_op jit(solution)/shard_map/all_to_all | solution.py:1061
  12.9 16.5 %collective-permute-start.1 = (f32[32,2048]{1,0:T(8,128)S(1)}, f32[32,2048]{1,0:T(8,128)S(1)}, u32[]{:S(2)}, u32[]{:S(2)}) collective-permute-start(f32[32,2048]{1,0:T(8,128)S(1)} %get-tuple-element.34), channel_id=1, source_target_pairs={{0,28},{4,0},{8,4},{12,8},{16,12},{20,16},{24,20},{28,24},{1,29},{... | collective-permute-start | bytes 786440 | tf_op jit(solution)/shard_map/ppermute | solution.py:1066
  17.7 11.7 %collective-permute-start = (f32[32,2048]{1,0:T(8,128)S(1)}, f32[32,2048]{1,0:T(8,128)S(1)}, u32[]{:S(2)}, u32[]{:S(2)}) collective-permute-start(f32[32,2048]{1,0:T(8,128)S(1)} %get-tuple-element.35), channel_id=1, source_target_pairs={{0,4},{4,8},{8,12},{12,16},{16,20},{20,24},{24,28},{28,0},{1,5},{5... | collective-permute-start | bytes 786440 | tf_op jit(solution)/shard_map/ppermute | solution.py:1065
  23.9 0.7 copy-start
  29.4 0.7 copy-start.1
  29.4 0.8 copy-start.2
where the time goes:
time: 173 us; the launch traced here: 171 us
  Pallas kernels  109 us (63%)
  blocking collectives  46 us (27%)
  starting transfers between devices  12.1 us (7%)
  local copies, waits for them, and re-layouts  2.58 us (1%)
    pallas_call x1, Pallas kernels, body(): pl.pallas_call(functools.partial(apply_kernel, first=True, **static), out...  38.7 us
    pallas_call x1, Pallas kernels, body(): pl.pallas_call(functools.partial(final_kernel, layout=layout, hold=hold,...  28.6 us
    all_to_all x1, blocking collectives, body(): lax.all_to_all(message, 'pencil', split_axis=0, concat_axis=0, tiled=True)  28.5 us
    pallas_call x1, Pallas kernels, body(): pl.pallas_call(functools.partial(apply_kernel, first=False, **static), ou...  27.6 us
    all_to_all x1, blocking collectives, body(): lax.all_to_all(sums, ('pencil', 'lev'), split_axis=0, concat_axis=0, tile...  17.6 us
    all_to_all x1, starting transfers between devices, body(): lax.all_to_all(packed, 'pencil', split_axis=0, concat_axis=0, tiled=True)  7.28 us
    pallas_call x1, Pallas kernels, body(): pl.pallas_call(functools.partial(bands_kernel, rows_block=row_size), out_...  6.27 us
    ppermute x1, starting transfers between devices, body(): std_r = lax.ppermute(std[:HALO, :], 'pencil', left)  4.77 us
  transfers between devices with their start and end apart: 3, of which 1 were waited for; matrix products, arithmetic and copies ran while one was open for 1% of the time, Pallas kernels for 6%

commit v1 on v0

--- a/solution.py
+++ b/solution.py
@@ -135,7 +135,7 @@
         )
         return carry
 
-    lax.fori_loop(0, parts, per_part, 0)
+    lax.fori_loop(0, parts, per_part, 0, unroll=parts <= GROUP)
 
 
 class Layout:
@@ -270,7 +270,7 @@
         line_sum[block_of] += total
         return carry
 
-    lax.fori_loop(0, senders, per_sender, 0)
+    lax.fori_loop(0, senders, per_sender, 0, unroll=senders <= GROUP)
 
     number = iota((stencil, LANES), 0).astype(F32)
     nowhere = float((height // LANES) * wide)
@@ -433,7 +433,7 @@
         info_out, merged_h = take(2)
     addr, wgt, start, lines_s, val = take(5)
     if first:
-        std_flat, picked, spread = take(3)
+        std_flat, picked, chosen = take(3)
     scale, merged, sums, high_s, low_s, std, std_l, std_r, lat2, lon2, field = take(11)
     copies = take(PAIR)
     sems, in_sems, out_sems, val_sem = take(4)
@@ -517,33 +517,9 @@
     known = own[...]
     column = 2 * stencil if first else 2 * stencil + 2
     scale[...] = jnp.broadcast_to(known[:, column : column + 1], (slots, LANES))
-    if first:
-        lane_f = iota((8, LANES), 1).astype(F32)
-
-        def build(i, carry):
-            top = pl.multiple_of(i * 8, 8)
-            info = own[pl.ds(top, 8), :]
-
-            def wide_of(at):
-                return jnp.broadcast_to(info[:, at : at + 1], (8, LANES))
-
-            rows = [None] * stencil
-            for k in range(stencil):
-                weight = wide_of(stencil + k)
-                code = wide_of(CODES + k)
-                spread[pl.ds(k * slots + top, 8), :] = jnp.where(
-                    lane_f == wide_of(k), weight, 0.0
-                )
-                for place in range(k + 1):
-                    term = jnp.where(lane_f + float(LANES * place) == code, weight, 0.0)
-                    rows[place] = term if rows[place] is None else rows[place] + term
-            for place in range(stencil):
-                merged[pl.ds(place * slots + top, 8), :] = rows[place]
-            return carry
-
-        lax.fori_loop(0, slots // 8, build, 0)
-        merged_copy.start()
     own_copy.wait()
+    if pending:
+        pending.pop(2).wait()
     if not first:
         merged_copy.wait()
 
@@ -565,6 +541,66 @@
 
     def batches_of(one, two):
         return jnp.maximum(own_line(one, stencil), own_line(two, stencil))
+
+    def own_groups(action):
+        def group_at(top):
+            top = pl.multiple_of(top, 8)
+            most = own_line(top, stencil)
+            for i in range(1, 8):
+                most = jnp.maximum(most, own_line(top + i, stencil))
+
+            @pl.when(most <= 1)
+            def _():
+                action(top, True)
+
+            @pl.when(most > 1)
+            def _():
+                action(top, False)
+
+        if capacity % 8 or chunks > 1:
+
+            def step(i, carry):
+                group_at(i * 8)
+                return carry
+
+            lax.fori_loop(0, slots // 8, step, 0)
+        else:
+
+            def per_sender(sender, carry):
+                amount = start_of(sender, me, 0, 1) - start_of(sender, me, 0, 0)
+
+                def step(i, inner):
+                    group_at(sender * capacity + i * 8)
+                    return inner
+
+                lax.fori_loop(0, lax.shift_right_logical(amount + 7, 3), step, 0)
+                return carry
+
+            lax.fori_loop(0, senders, per_sender, 0)
+
+    lane_f = iota((8, LANES), 1).astype(F32)
+
+    def columns_of(info, begin):
+        return [
+            jnp.broadcast_to(info[:, begin + k : begin + k + 1], (8, LANES))
+            for k in range(stencil)
+        ]
+
+    def build(top, short):
+        info = own[pl.ds(top, 8), :]
+        codes = columns_of(info, CODES)
+        weights = columns_of(info, stencil)
+        for place in range(stencil):
+            row = jnp.zeros((8, LANES), F32)
+            if place < BATCH or not short:
+                at = lane_f + float(LANES * place)
+                for k in range(place, stencil):
+                    row = row + jnp.where(at == codes[k], weights[k], 0.0)
+            merged[pl.ds(place * slots + top, 8), :] = row
+
+    if first:
+        own_groups(build)
+        merged_copy.start()
 
     def own_pairs(chunk, action):
         def per_sender(sender, carry):
@@ -625,6 +661,8 @@
 
     def scatter_chunk(chunk):
         scatter_own(chunk)
+        for copy in pending:
+            copy.wait()
         scatter_halo(chunk)
 
     def over_chunks(work):
@@ -639,8 +677,6 @@
 
             lax.fori_loop(0, chunks, step, 0)
 
-    for copy in pending:
-        copy.wait()
     if not first:
         each_owner(lambda copy: copy.wait())
     over_chunks(scatter_chunk)
@@ -703,6 +739,10 @@
                         line = own_line(slot, begin + j)
                         row = merged[pl.ds((begin + j) * slots + slot, 1), :]
                         terms.append(row * smoothed[pl.ds(line, 1), :])
+                        if first:
+                            picked[pl.ds((begin + j) * slots + slot, 1), :] = std_flat[
+                                pl.ds(line, 1), :
+                            ]
                     result.append(total + ((terms[0] + terms[1]) + (terms[2] + terms[3])))
                 return tuple(result)
 
@@ -718,31 +758,25 @@
 
         own_pairs(chunk, action)
 
-        if first:
-
-            def per_sender(sender, carry):
-                begin = start_of(sender, me, 0, 0)
-                amount = start_of(sender, me, 0, 1) - begin
-                base = (chunk * group + sender) * capacity
-
-                def pick(idx):
-                    slot = base + idx - begin
-                    at = spot(sender, idx, per, stencil)
-                    for k in range(stencil):
-                        line = lax.shift_right_logical(addr[at + k * LANES], 7)
-                        row = spread[pl.ds(k * slots + slot, 1), :]
-                        picked[pl.ds(k * slots + slot, 1), :] = row * std_flat[pl.ds(line, 1), :]
-
-                def both(one, two, has_two):
-                    pick(one)
-                    pick(two)
-
-                pairs(begin, begin + amount, both)
-                return carry
-
-            lax.fori_loop(0, group, per_sender, 0)
-
     over_chunks(gather_chunk)
+
+    def pick(top, short):
+        info = own[pl.ds(top, 8), :]
+        codes = columns_of(info, CODES)
+        places = BATCH if short else stencil
+        rows = [picked[pl.ds(place * slots + top, 8), :] for place in range(places)]
+        result = jnp.zeros((8, LANES), F32)
+        for k in range(stencil):
+            cell = jnp.zeros((8, LANES), F32)
+            for place in range(min(k + 1, places)):
+                at = lane_f + float(LANES * place)
+                cell = jnp.where(at == codes[k], rows[place], cell)
+            cell = jnp.sum(cell, axis=1, keepdims=True)
+            result = jnp.where(lane_f == float(stencil + k), cell, result)
+        chosen[pl.ds(top, 8), :] = result * info
+
+    if first:
+        own_groups(pick)
 
     def whole(x):
         return jnp.sum(x, axis=0, keepdims=True)
@@ -766,16 +800,10 @@
             )
         )
         message.append(jnp.zeros((8 - len(message), LANES), F32))
-        ones = jnp.ones((8, LANES), BF)
+        factors = chosen[...].T
         for k in range(stencil):
-            row = None
-            for part in split3(picked[k * slots : (k + 1) * slots, :]):
-                term = lax.dot_general(
-                    ones, part, (((1,), (1,)), ((), ())), preferred_element_type=F32
-                )
-                row = term if row is None else row + term
-            for i in range(lines):
-                message.append(row[0:1, i * LANES : (i + 1) * LANES])
+            row = factors[stencil + k : stencil + k + 1, :]
+            message += [row[:, i * LANES : (i + 1) * LANES] for i in range(lines)]
         message = jnp.concatenate(message, axis=0)
     else:
         slab = jnp.sum(replies[:, 0:8, :], axis=0)[lines : lines + 1, :]
@@ -1170,7 +1198,7 @@
             pltpu.SMEM((line,), F32),
             acc,
             pltpu.VMEM((stencil * slots, LANES), F32),
-            pltpu.VMEM((stencil * slots, LANES), F32),
+            column_slots,
         ]
         + work,
         compiler_params=params(),

time: 173 us -> 168 us (0.971); the launches traced: 171 us -> 169 us
  Pallas kernels: 109 us -> 102 us
  blocking collectives: 46 us -> 49.2 us
    pallas_call x1, Pallas kernels: 38.7 us -> 34.1 us  [body(): pl.pallas_call(functools.partial(apply_kernel, first=True, **static), out...]
    all_to_all x1, blocking collectives: 28.5 us -> 31.4 us  [body(): lax.all_to_all(message, 'pencil', split_axis=0, concat_axis=0, tiled=True)]
  transfers between devices with their start and end apart: 3 -> 3, of which waited for: 1 -> 1; matrix products, arithmetic and copies ran while one was open for 1% -> 1% of each run, Pallas kernels for 6% -> 5%
where the time goes in v1:
time: 168 us; the launch traced here: 169 us
  Pallas kernels  102 us (61%)
  blocking collectives  49.2 us (29%)
  starting transfers between devices  12.1 us (7%)
  local copies, waits for them, and re-layouts  2.58 us (2%)
  waiting for transfers between devices  1.99 us (1%)
    pallas_call x1, Pallas kernels, body(): pl.pallas_call(functools.partial(apply_kernel, first=True, **static), out...  34.1 us
    all_to_all x1, blocking collectives, body(): lax.all_to_all(message, 'pencil', split_axis=0, concat_axis=0, tiled=True)  31.4 us
    pallas_call x1, Pallas kernels, body(): pl.pallas_call(functools.partial(final_kernel, layout=layout, hold=hold,...  28.7 us
    pallas_call x1, Pallas kernels, body(): pl.pallas_call(functools.partial(apply_kernel, first=False, **static), ou...  28 us
    all_to_all x1, blocking collectives, body(): lax.all_to_all(sums, ('pencil', 'lev'), split_axis=0, concat_axis=0, tile...  17.9 us
    all_to_all x1, starting transfers between devices, body(): lax.all_to_all(packed, 'pencil', split_axis=0, concat_axis=0, tiled=True)  7.28 us
    pallas_call x1, Pallas kernels, body(): pl.pallas_call(functools.partial(bands_kernel, rows_block=row_size), out_...  6.27 us
    ppermute x1, starting transfers between devices, body(): std_r = lax.ppermute(std[:HALO, :], 'pencil', left)  4.77 us
  transfers between devices with their start and end apart: 3, of which 1 were waited for; matrix products, arithmetic and copies ran while one was open for 1% of the time, Pallas kernels for 5%

profile of v1, /device:TPU:0, one launch (start us, length us, event | category | flops | bytes accessed | tf_op | source)
XLA Modules:
  0.0 169.5 jit_solution(15637349105046298823)
XLA Ops:
  1.3 2.3 %pack.1 = f32[8,40,256]{2,1,0:T(8,128)} custom-call(s32[1]{0:T(128)S(6)} %copy.11.counts, s32[1,256]{1,0:T(1,128)} %bitcast.36, s32[16,256]{1,0:T(8,128)} %bitcast.34, f32[16,256]{1,0:T(8,128)} %bitcast.35, f32[1,256]{1,0:T(1,128)} %bitcast.37, f32[1,256]{1,0:T(1,128)} %bitcast.38), custom_call_target="tpu_custom_call" | custom-call | tf_op jit(solution)/shard_map/pack/pallas_call | solution.py:1072
  3.6 7.3 %all-to-all-start = ((f32[8,40,256]{2,1,0:T(8,128)}), f32[8,40,256]{2,1,0:T(8,128)S(1)}, u32[]{:S(2)}, u32[]{:S(2)}) async-start(f32[8,40,256]{2,1,0:T(8,128)} %pack.1), calls=%async_computation | async-start | bytes 655360 | tf_op jit(solution)/shard_map/all_to_all | solution.py:1089
  10.9 1.1 slice_bitcast_fusion
  12.0 4.8 %collective-permute-start.1 = (f32[32,2048]{1,0:T(8,128)S(1)}, f32[32,2048]{1,0:T(8,128)S(1)}, u32[]{:S(2)}, u32[]{:S(2)}) collective-permute-start(f32[32,2048]{1,0:T(8,128)S(1)} %get-tuple-element.34), channel_id=1, source_target_pairs={{0,28},{4,0},{8,4},{12,8},{16,12},{20,16},{24,20},{28,24},{1,29},{... | collective-permute-start | bytes 786440 | tf_op jit(solution)/shard_map/ppermute | solution.py:1094
  16.7 0.0 collective-permute-start
  16.8 6.3 %bands.1 = (bf16[2,3,512,256]{3,2,1,0:T(8,128)(2,1)}, bf16[2,192,256]{2,1,0:T(8,128)(2,1)}, bf16[2,128,160]{2,1,0:T(8,128)(2,1)}, bf16[2,512,256]{2,1,0:T(8,128)(2,1)}) custom-call(f32[31]{0:T(128)} %bitcast.41, f32[31]{0:T(128)} %bitcast.42), custom_call_target="tpu_custom_call" | custom-call | tf_op jit(solution)/shard_map/bands/pallas_call | solution.py:1098
  23.0 0.0 all-to-all-done.recv
  23.0 0.0 copy-start
  23.0 0.7 copy-done
  23.8 2.8 %unpack.1 = (s32[592,128]{1,0:T(8,128)}, f32[272,128]{1,0:T(8,128)}, s32[96,128]{1,0:T(8,128)}, f32[512,128]{1,0:T(8,128)}) custom-call(s32[1]{0:T(128)} %bitcast.meta.refs_0_, f32[8,40,256]{2,1,0:T(8,128)} %copy-done), custom_call_target="tpu_custom_call" | custom-call | tf_op jit(solution)/shard_map/unpack/pallas_call | solution.py:1113
  26.5 2.0 %collective-permute-done.1.refs_7_.refs_9_ = f32[32,2048]{1,0:T(8,128)S(1)} collective-permute-done((f32[32,2048]{1,0:T(8,128)S(1)}, f32[32,2048]{1,0:T(8,128)S(1)}, u32[]{:S(2)}, u32[]{:S(2)}) %collective-permute-start.1) | collective-permute-done | bytes 262176 | tf_op jit(solution)/shard_map/ppermute | solution.py:1094
  28.5 0.0 copy-start.1
  28.5 0.0 collective-permute-done.refs_6_.refs_8_
  28.5 0.0 copy-start.2
  28.5 0.7 copy-done.1
  29.2 0.1 copy-done.2
  29.3 34.1 %apply_first.1 = (f32[512,2048]{1,0:T(8,128)}, f32[8,72,128]{2,1,0:T(8,128)}, f32[512,128]{1,0:T(8,128)}, f32[8192,128]{1,0:T(8,128)}) custom-call(s32[1]{0:T(128)} %bitcast.meta.refs_0_, s32[75776]{0:T(1024)} %bitcast.25, f32[34816]{0:T(1024)} %bitcast.28, s32[12288]{0:T(1024)} %bitcast.32, f32[512,128]{1,0:T(8,128)} %get-tuple-element.21.refs_4_, ...), custom_call_target="tpu_custom_call" | custom-call | tf_op jit(solution)/shard_map/apply_first/pallas_call | solution.py:1186
  63.4 31.4 %all_to_all.15.refs_6_ = f32[8,72,128]{2,1,0:T(8,128)} all-to-all(f32[8,72,128]{2,1,0:T(8,128)} %get-tuple-element.24), channel_id=1, replica_groups=mesh['pencil'=8,'lev'=4] {'pencil'}, dimensions={0} | all-to-all | bytes 589824 | tf_op jit(solution)/shard_map/all_to_all | solution.py:1208
  94.8 28.0 %apply_second.1 = (f32[512,2048]{1,0:T(8,128)}, f32[32,8,128]{2,1,0:T(8,128)}) custom-call(s32[1]{0:T(128)} %bitcast.meta.refs_0_, s32[75776]{0:T(1024)} %bitcast.26, f32[34816]{0:T(1024)} %bitcast.29, s32[12288]{0:T(1024)} %bitcast.33, f32[512,128]{1,0:T(8,128)} %get-tuple-element.25.refs_4_, f32[73728]{0:T(1024)} %bitcast.23, ...), custom_call_target="tpu_custom_call" | custom-call | tf_op jit(solution)/shard_map/apply_second/pallas_call | solution.py:1211
  122.8 17.9 %all_to_all.16 = f32[32,8,128]{2,1,0:T(8,128)} all-to-all(f32[32,8,128]{2,1,0:T(8,128)} %get-tuple-element.27), channel_id=1, replica_groups=mesh['pencil'=8,'lev'=4] {'pencil','lev'}, dimensions={0} | all-to-all | bytes 262144 | tf_op jit(solution)/shard_map/all_to_all | solution.py:1238
  140.6 28.7 %outputs.1 = (f32[256,4096]{1,0:T(8,128)}, f32[512,2048]{1,0:T(8,128)}) custom-call(s32[75776]{0:T(1024)} %bitcast.27, f32[34816]{0:T(1024)} %bitcast.30, f32[73728]{0:T(1024)} %bitcast.24, f32[8,4,8,128]{3,2,1,0:T(8,128)} %bitcast.31, f32[512,2048]{1,0:T(8,128)} %bitcast.22, f32[512,2048]{1,0:T(8,128)} %get-tuple-element.28.field0_h, ...), custom_call_target="tpu_custom_call" | custom-call | tf_op jit(solution)/shard_map/outputs/pallas_call | solution.py:1250
Async XLA Ops:
  3.6 19.4 %all-to-all-start = ((f32[8,40,256]{2,1,0:T(8,128)}), f32[8,40,256]{2,1,0:T(8,128)S(1)}, u32[]{:S(2)}, u32[]{:S(2)}) async-start(f32[8,40,256]{2,1,0:T(8,128)} %pack.1), calls=%async_computation | async-start | bytes 655360 | tf_op jit(solution)/shard_map/all_to_all | solution.py:1089
  12.0 16.5 %collective-permute-start.1 = (f32[32,2048]{1,0:T(8,128)S(1)}, f32[32,2048]{1,0:T(8,128)S(1)}, u32[]{:S(2)}, u32[]{:S(2)}) collective-permute-start(f32[32,2048]{1,0:T(8,128)S(1)} %get-tuple-element.34), channel_id=1, source_target_pairs={{0,28},{4,0},{8,4},{12,8},{16,12},{20,16},{24,20},{28,24},{1,29},{... | collective-permute-start | bytes 786440 | tf_op jit(solution)/shard_map/ppermute | solution.py:1094
  16.7 11.7 %collective-permute-start = (f32[32,2048]{1,0:T(8,128)S(1)}, f32[32,2048]{1,0:T(8,128)S(1)}, u32[]{:S(2)}, u32[]{:S(2)}) collective-permute-start(f32[32,2048]{1,0:T(8,128)S(1)} %get-tuple-element.35), channel_id=1, source_target_pairs={{0,4},{4,8},{8,12},{12,16},{16,20},{20,24},{24,28},{28,0},{1,5},{5... | collective-permute-start | bytes 786440 | tf_op jit(solution)/shard_map/ppermute | solution.py:1093
  23.0 0.7 copy-start
  28.5 0.7 copy-start.1
  28.5 0.8 copy-start.2

commit v2 on v1

--- a/solution.py
+++ b/solution.py
@@ -21,6 +21,7 @@
 COPIES = 4
 PAIR = 2
 BATCH = 4
+BLOCK = 32
 CODES = 40
 VMEM_LIMIT = 58 * 1024 * 1024
 
@@ -35,6 +36,10 @@
 
 def hbm():
     return pl.BlockSpec(memory_space=pl.ANY)
+
+
+def cost(nanoseconds):
+    return pl.CostEstimate(flops=0, bytes_accessed=3690 * nanoseconds, transcendentals=0)
 
 
 def params():
@@ -59,7 +64,7 @@
 
 def mm_parts(a_parts, b_parts):
     (ah, al), (bh, bl) = a_parts, b_parts
-    return mm(ah, bh) + (mm(al, bh) + mm(ah, bl))
+    return mm(jnp.concatenate([ah, al, ah], axis=1), jnp.concatenate([bh, bh, bl], axis=0))
 
 
 def iota(shape, dim):
@@ -299,7 +304,16 @@
         lists = jnp.concatenate(lists, axis=0).astype(I32)
         top = i * (stencil + 8)
         own_lines[top : top + stencil, :] = lists
-        own_lines[top + stencil : top + stencil + 8, :] = jnp.broadcast_to(batches, (8, LANES))
+        batches = batches.astype(F32)
+        most = jnp.zeros((1, LANES), F32)
+        slot = iota((1, LANES), 1)
+        for begin in range(0, LANES, BLOCK):
+            here = (slot >= begin) & (slot < begin + BLOCK)
+            found = jnp.max(jnp.where(here, batches, 0.0), axis=1, keepdims=True)
+            most = jnp.where(here, found, most)
+        own_lines[top + stencil : top + stencil + 8, :] = jnp.where(
+            iota((8, LANES), 0) == 0, batches, most
+        ).astype(I32)
         codes = jnp.concatenate(
             [
                 jnp.zeros((CODES, LANES), F32),
@@ -486,6 +500,11 @@
     ]
     own_copy = pltpu.make_async_copy(own_lines, lines_s, in_sems.at[5])
     own_copy.start()
+    merged_copy = pltpu.make_async_copy(
+        *((merged, merged_h) if first else (merged_h, merged)), in_sems.at[6]
+    )
+    if not first:
+        merged_copy.start()
     for copy in operands:
         copy.start()
 
@@ -506,12 +525,6 @@
         each_owner(lambda copy: copy.start())
     zero_all(copies)
     zero_all([sums])
-
-    merged_copy = pltpu.make_async_copy(
-        *((merged, merged_h) if first else (merged_h, merged)), in_sems.at[6]
-    )
-    if not first:
-        merged_copy.start()
 
     lane_of = iota((slots, LANES), 1)
     known = own[...]
@@ -545,58 +558,56 @@
     def own_groups(action):
         def group_at(top):
             top = pl.multiple_of(top, 8)
-            most = own_line(top, stencil)
-            for i in range(1, 8):
-                most = jnp.maximum(most, own_line(top + i, stencil))
-
-            @pl.when(most <= 1)
+            most = own_line(top, stencil + 1)
+
+            @pl.when(most <= 2)
             def _():
-                action(top, True)
-
-            @pl.when(most > 1)
+                action(top, 2 * BATCH)
+
+            @pl.when(most > 2)
             def _():
-                action(top, False)
-
-        if capacity % 8 or chunks > 1:
+                action(top, stencil)
+
+        if capacity % BLOCK or chunks > 1:
 
             def step(i, carry):
-                group_at(i * 8)
+                group_at(i * BLOCK)
                 return carry
 
-            lax.fori_loop(0, slots // 8, step, 0)
+            lax.fori_loop(0, slots // BLOCK, step, 0)
         else:
 
             def per_sender(sender, carry):
                 amount = start_of(sender, me, 0, 1) - start_of(sender, me, 0, 0)
 
                 def step(i, inner):
-                    group_at(sender * capacity + i * 8)
+                    group_at(sender * capacity + i * BLOCK)
                     return inner
 
-                lax.fori_loop(0, lax.shift_right_logical(amount + 7, 3), step, 0)
+                lax.fori_loop(0, lax.div(amount + (BLOCK - 1), BLOCK), step, 0)
                 return carry
 
             lax.fori_loop(0, senders, per_sender, 0)
 
-    lane_f = iota((8, LANES), 1).astype(F32)
+    lane_f = iota((BLOCK, LANES), 1).astype(F32)
 
     def columns_of(info, begin):
         return [
-            jnp.broadcast_to(info[:, begin + k : begin + k + 1], (8, LANES))
+            jnp.broadcast_to(info[:, begin + k : begin + k + 1], (BLOCK, LANES))
             for k in range(stencil)
         ]
 
-    def build(top, short):
-        info = own[pl.ds(top, 8), :]
+    def build(top, places):
+        info = own[pl.ds(top, BLOCK), :]
         codes = columns_of(info, CODES)
         weights = columns_of(info, stencil)
         for place in range(stencil):
-            row = jnp.zeros((8, LANES), F32)
-            if place < BATCH or not short:
+            row = jnp.zeros((BLOCK, LANES), F32)
+            if place < places:
                 at = lane_f + float(LANES * place)
                 for k in range(place, stencil):
                     row = row + jnp.where(at == codes[k], weights[k], 0.0)
-            merged[pl.ds(place * slots + top, 8), :] = row
+            merged[pl.ds(place * slots + top, BLOCK), :] = row
 
     if first:
         own_groups(build)
@@ -760,20 +771,19 @@
 
     over_chunks(gather_chunk)
 
-    def pick(top, short):
-        info = own[pl.ds(top, 8), :]
+    def pick(top, places):
+        info = own[pl.ds(top, BLOCK), :]
         codes = columns_of(info, CODES)
-        places = BATCH if short else stencil
-        rows = [picked[pl.ds(place * slots + top, 8), :] for place in range(places)]
-        result = jnp.zeros((8, LANES), F32)
+        rows = [picked[pl.ds(place * slots + top, BLOCK), :] for place in range(places)]
+        result = jnp.zeros((BLOCK, LANES), F32)
         for k in range(stencil):
-            cell = jnp.zeros((8, LANES), F32)
+            cell = jnp.zeros((BLOCK, LANES), F32)
             for place in range(min(k + 1, places)):
                 at = lane_f + float(LANES * place)
                 cell = jnp.where(at == codes[k], rows[place], cell)
             cell = jnp.sum(cell, axis=1, keepdims=True)
             result = jnp.where(lane_f == float(stencil + k), cell, result)
-        chosen[pl.ds(top, 8), :] = result * info
+        chosen[pl.ds(top, BLOCK), :] = result * info
 
     if first:
         own_groups(pick)
@@ -1077,6 +1087,7 @@
         in_specs=[smem()] + [vmem()] * 5,
         out_specs=vmem(),
         compiler_params=params(),
+        cost_estimate=cost(12000),
         name="pack",
     )(
         obs_counts,
@@ -1106,6 +1117,7 @@
         in_specs=[smem(), smem()],
         out_specs=[vmem()] * 4,
         compiler_params=params(),
+        cost_estimate=cost(6000),
         name="bands",
     )(x_kernel[0], y_kernel[0])
 
@@ -1135,6 +1147,7 @@
             pltpu.VMEM((slots // LANES, stencil, LANES), F32),
         ],
         compiler_params=params(),
+        cost_estimate=cost(100),
         name="unpack",
     )(meta, recv)
     ints = ints.reshape(-1)

time: 168 us -> 164 us (0.976); the launches traced: 169 us -> 164 us
  Pallas kernels: 102 us -> 94.9 us
    all_to_all x1, blocking collectives: 17.9 us -> 22.3 us  [body(): lax.all_to_all(sums, ('pencil', 'lev'), split_axis=0, concat_axis=0, tile...]
    pallas_call x1, Pallas kernels: 34.1 us -> 30.3 us  [body(): pl.pallas_call(functools.partial(apply_kernel, first=True, **static), out...]
    pallas_call x1, Pallas kernels: 28 us -> 24.8 us  [body(): pl.pallas_call(functools.partial(apply_kernel, first=False, **static), ou...]
    all_to_all x1, blocking collectives: 31.4 us -> 28.3 us  [body(): lax.all_to_all(message, 'pencil', split_axis=0, concat_axis=0, tiled=True)]
  transfers between devices with their start and end apart: 3 -> 3, of which waited for: 1 -> 1; matrix products, arithmetic and copies ran while one was open for 1% -> 1% of each run, Pallas kernels for 5% -> 6%
where the time goes in v2:
time: 164 us
  Pallas kernels  94.9 us (58%)
  blocking collectives  50.7 us (31%)
  starting transfers between devices  12.1 us (7%)
  local copies, waits for them, and re-layouts  2.58 us (2%)
  waiting for transfers between devices  1.95 us (1%)
    pallas_call x1, Pallas kernels, body(): pl.pallas_call(functools.partial(apply_kernel, first=True, **static), out...  30.3 us
    pallas_call x1, Pallas kernels, body(): pl.pallas_call(functools.partial(final_kernel, layout=layout, hold=hold,...  28.4 us
    all_to_all x1, blocking collectives, body(): lax.all_to_all(message, 'pencil', split_axis=0, concat_axis=0, tiled=True)  28.3 us
    pallas_call x1, Pallas kernels, body(): pl.pallas_call(functools.partial(apply_kernel, first=False, **static), ou...  24.8 us
    all_to_all x1, blocking collectives, body(): lax.all_to_all(sums, ('pencil', 'lev'), split_axis=0, concat_axis=0, tile...  22.3 us
    all_to_all x1, starting transfers between devices, body(): lax.all_to_all(packed, 'pencil', split_axis=0, concat_axis=0, tiled=True)  7.28 us
    pallas_call x1, Pallas kernels, body(): pl.pallas_call(functools.partial(bands_kernel, rows_block=row_size), out_...  6.27 us
    ppermute x1, starting transfers between devices, body(): std_r = lax.ppermute(std[:HALO, :], 'pencil', left)  4.77 us
  transfers between devices with their start and end apart: 3, of which 1 were waited for; matrix products, arithmetic and copies ran while one was open for 1% of the time, Pallas kernels for 6%

profile of v2, /device:TPU:0, one launch (start us, length us, event | category | flops | bytes accessed | tf_op | source)
XLA Modules:
  0.0 163.7 jit_solution(16521150347671237441)
XLA Ops:
  1.3 2.3 %pack.1 = f32[8,40,256]{2,1,0:T(8,128)} custom-call(s32[1]{0:T(128)S(6)} %copy.11.counts, s32[1,256]{1,0:T(1,128)} %bitcast.36, s32[16,256]{1,0:T(8,128)} %bitcast.34, f32[16,256]{1,0:T(8,128)} %bitcast.35, f32[1,256]{1,0:T(1,128)} %bitcast.37, f32[1,256]{1,0:T(1,128)} %bitcast.38), custom_call_target="tpu_custom_call" | custom-call | bytes 44280000 | tf_op jit(solution)/shard_map/pack/pallas_call | solution.py:1082
  3.6 7.3 %all-to-all-start = ((f32[8,40,256]{2,1,0:T(8,128)}), f32[8,40,256]{2,1,0:T(8,128)S(1)}, u32[]{:S(2)}, u32[]{:S(2)}) async-start(f32[8,40,256]{2,1,0:T(8,128)} %pack.1), calls=%async_computation | async-start | bytes 655360 | tf_op jit(solution)/shard_map/all_to_all | solution.py:1100
  10.9 1.1 slice_bitcast_fusion
  12.0 4.8 %collective-permute-start.1 = (f32[32,2048]{1,0:T(8,128)S(1)}, f32[32,2048]{1,0:T(8,128)S(1)}, u32[]{:S(2)}, u32[]{:S(2)}) collective-permute-start(f32[32,2048]{1,0:T(8,128)S(1)} %get-tuple-element.34), channel_id=1, source_target_pairs={{0,28},{4,0},{8,4},{12,8},{16,12},{20,16},{24,20},{28,24},{1,29},{... | collective-permute-start | bytes 786440 | tf_op jit(solution)/shard_map/ppermute | solution.py:1105
  16.7 0.0 collective-permute-start
  16.8 6.3 %bands.1 = (bf16[2,3,512,256]{3,2,1,0:T(8,128)(2,1)}, bf16[2,192,256]{2,1,0:T(8,128)(2,1)}, bf16[2,128,160]{2,1,0:T(8,128)(2,1)}, bf16[2,512,256]{2,1,0:T(8,128)(2,1)}) custom-call(f32[31]{0:T(128)} %bitcast.41, f32[31]{0:T(128)} %bitcast.42), custom_call_target="tpu_custom_call" | custom-call | bytes 22140000 | tf_op jit(solution)/shard_map/bands/pallas_call | solution.py:1109
  23.0 0.0 all-to-all-done.recv
  23.0 0.0 copy-start
  23.0 0.7 copy-done
  23.8 2.8 %unpack.1 = (s32[592,128]{1,0:T(8,128)}, f32[272,128]{1,0:T(8,128)}, s32[96,128]{1,0:T(8,128)}, f32[512,128]{1,0:T(8,128)}) custom-call(s32[1]{0:T(128)} %bitcast.meta.refs_0_, f32[8,40,256]{2,1,0:T(8,128)} %copy-done), custom_call_target="tpu_custom_call" | custom-call | bytes 369000 | tf_op jit(solution)/shard_map/unpack/pallas_call | solution.py:1125
  26.5 1.9 %collective-permute-done.1.refs_7_.refs_9_ = f32[32,2048]{1,0:T(8,128)S(1)} collective-permute-done((f32[32,2048]{1,0:T(8,128)S(1)}, f32[32,2048]{1,0:T(8,128)S(1)}, u32[]{:S(2)}, u32[]{:S(2)}) %collective-permute-start.1) | collective-permute-done | bytes 262176 | tf_op jit(solution)/shard_map/ppermute | solution.py:1105
  28.5 0.0 copy-start.1
  28.5 0.0 collective-permute-done.refs_6_.refs_8_
  28.5 0.0 copy-start.2
  28.5 0.7 copy-done.1
  29.2 0.1 copy-done.2
  29.3 30.3 %apply_first.1 = (f32[512,2048]{1,0:T(8,128)}, f32[8,72,128]{2,1,0:T(8,128)}, f32[512,128]{1,0:T(8,128)}, f32[8192,128]{1,0:T(8,128)}) custom-call(s32[1]{0:T(128)} %bitcast.meta.refs_0_, s32[75776]{0:T(1024)} %bitcast.25, f32[34816]{0:T(1024)} %bitcast.28, s32[12288]{0:T(1024)} %bitcast.32, f32[512,128]{1,0:T(8,128)} %get-tuple-element.21.refs_4_, ...), custom_call_target="tpu_custom_call" | custom-call | tf_op jit(solution)/shard_map/apply_first/pallas_call | solution.py:1199
  59.6 28.3 %all_to_all.15.refs_6_ = f32[8,72,128]{2,1,0:T(8,128)} all-to-all(f32[8,72,128]{2,1,0:T(8,128)} %get-tuple-element.24), channel_id=1, replica_groups=mesh['pencil'=8,'lev'=4] {'pencil'}, dimensions={0} | all-to-all | bytes 589824 | tf_op jit(solution)/shard_map/all_to_all | solution.py:1221
  87.9 24.8 %apply_second.1 = (f32[512,2048]{1,0:T(8,128)}, f32[32,8,128]{2,1,0:T(8,128)}) custom-call(s32[1]{0:T(128)} %bitcast.meta.refs_0_, s32[75776]{0:T(1024)} %bitcast.26, f32[34816]{0:T(1024)} %bitcast.29, s32[12288]{0:T(1024)} %bitcast.33, f32[512,128]{1,0:T(8,128)} %get-tuple-element.25.refs_4_, f32[73728]{0:T(1024)} %bitcast.23, ...), custom_call_target="tpu_custom_call" | custom-call | tf_op jit(solution)/shard_map/apply_second/pallas_call | solution.py:1224
  112.8 22.3 %all_to_all.16 = f32[32,8,128]{2,1,0:T(8,128)} all-to-all(f32[32,8,128]{2,1,0:T(8,128)} %get-tuple-element.27), channel_id=1, replica_groups=mesh['pencil'=8,'lev'=4] {'pencil','lev'}, dimensions={0} | all-to-all | bytes 262144 | tf_op jit(solution)/shard_map/all_to_all | solution.py:1251
  135.1 28.4 %outputs.1 = (f32[256,4096]{1,0:T(8,128)}, f32[512,2048]{1,0:T(8,128)}) custom-call(s32[75776]{0:T(1024)} %bitcast.27, f32[34816]{0:T(1024)} %bitcast.30, f32[73728]{0:T(1024)} %bitcast.24, f32[8,4,8,128]{3,2,1,0:T(8,128)} %bitcast.31, f32[512,2048]{1,0:T(8,128)} %bitcast.22, f32[512,2048]{1,0:T(8,128)} %get-tuple-element.28.field0_h, ...), custom_call_target="tpu_custom_call" | custom-call | tf_op jit(solution)/shard_map/outputs/pallas_call | solution.py:1263
Async XLA Ops:
  3.6 19.4 %all-to-all-start = ((f32[8,40,256]{2,1,0:T(8,128)}), f32[8,40,256]{2,1,0:T(8,128)S(1)}, u32[]{:S(2)}, u32[]{:S(2)}) async-start(f32[8,40,256]{2,1,0:T(8,128)} %pack.1), calls=%async_computation | async-start | bytes 655360 | tf_op jit(solution)/shard_map/all_to_all | solution.py:1100
  12.0 16.5 %collective-permute-start.1 = (f32[32,2048]{1,0:T(8,128)S(1)}, f32[32,2048]{1,0:T(8,128)S(1)}, u32[]{:S(2)}, u32[]{:S(2)}) collective-permute-start(f32[32,2048]{1,0:T(8,128)S(1)} %get-tuple-element.34), channel_id=1, source_target_pairs={{0,28},{4,0},{8,4},{12,8},{16,12},{20,16},{24,20},{28,24},{1,29},{... | collective-permute-start | bytes 786440 | tf_op jit(solution)/shard_map/ppermute | solution.py:1105
  16.7 11.7 %collective-permute-start = (f32[32,2048]{1,0:T(8,128)S(1)}, f32[32,2048]{1,0:T(8,128)S(1)}, u32[]{:S(2)}, u32[]{:S(2)}) collective-permute-start(f32[32,2048]{1,0:T(8,128)S(1)} %get-tuple-element.35), channel_id=1, source_target_pairs={{0,4},{4,8},{8,12},{12,16},{16,20},{20,24},{24,28},{28,0},{1,5},{5... | collective-permute-start | bytes 786440 | tf_op jit(solution)/shard_map/ppermute | solution.py:1104
  23.0 0.7 copy-start
  28.5 0.7 copy-start.1
  28.5 0.8 copy-start.2

commit v3 on v2

--- a/solution.py
+++ b/solution.py
@@ -216,8 +216,13 @@
     lane_sum[...] = jnp.zeros(lane_sum.shape, F32)
     place = iota((LANES, hold), 0)
     index = iota((LANES, hold), 1)
+    lane = iota((1, LANES), 1)
+    halo_block = slots // LANES
+    after = lax.rem(me + 1, parts)
+    ahead = lax.rem(me + parts - 1, parts)
 
     def per_sender(sender, carry):
+        halo_before, amounts = carry
         cell = recv[sender, 0:stencil, :].astype(I32)
         tail = recv[sender, 2 * stencil : 2 * stencil + 8, :]
         whole = tail.astype(I32)
@@ -252,35 +257,58 @@
         put(floats, layout.floats["wgt"], sender, recv[sender, stencil : 2 * stencil, :])
         put(floats, layout.floats["val"], sender, tail[0:1, :])
 
-        here = iota((1, LANES), 1) == me
-        begin = jnp.sum(jnp.where(here, whole[5:6, :LANES], 0), axis=1, keepdims=True)
-        end = jnp.sum(jnp.where(here, whole[5:6, LANES : 2 * LANES], 0), axis=1, keepdims=True)
+        def bound(line, half, owner):
+            part = whole[5 + line : 6 + line, half * LANES : (half + 1) * LANES]
+            return jnp.sum(jnp.where(lane == owner, part, 0), axis=1, keepdims=True)
+
+        at_lane = (addr & (LANES - 1)).astype(F32)
+        fields = jnp.concatenate([at_lane, recv[sender, stencil : 2 * stencil + 8, :]], axis=0)
+        fields = split3(fields)
+        back = owner * slots + sender * capacity + pos
+        lines_of = jnp.concatenate([right(addr, 7), back, jnp.zeros((7, hold), I32)], axis=0)
+        lines_of = split3(lines_of.astype(F32))
+
+        def gather_into(block_of, chosen):
+            select = jnp.where(chosen, 1.0, 0.0).astype(BF)
+            total = None
+            for part in fields:
+                term = nt(select, part)
+                total = term if total is None else total + term
+            own_sum[block_of, :, 0:CODES] += total
+            lane_sum[block_of] += nt(at_lane.astype(BF), select)
+            total = None
+            for part in lines_of:
+                term = nt(part, select)
+                total = term if total is None else total + term
+            line_sum[block_of] += total
+
+        begin, end = bound(0, 0, me), bound(0, 1, me)
         first_slot = sender * capacity
         block_of = first_slot // LANES
         within = place - (first_slot - block_of * LANES)
-        chosen = (within >= 0) & (index == begin + within) & (index < end)
-        select = jnp.where(chosen, 1.0, 0.0).astype(BF)
-        at_lane = (addr & (LANES - 1)).astype(F32)
-        fields = jnp.concatenate([at_lane, recv[sender, stencil : 2 * stencil + 8, :]], axis=0)
-        total = None
-        for part in split3(fields):
-            term = nt(select, part)
-            total = term if total is None else total + term
-        own_sum[block_of, :, 0:CODES] += total
-        lane_sum[block_of] += nt(at_lane.astype(BF), select)
-        total = None
-        for part in split2(right(addr, 7).astype(F32)):
-            term = nt(part, select)
-            total = term if total is None else total + term
-        line_sum[block_of] += total
-        return carry
-
-    lax.fori_loop(0, senders, per_sender, 0, unroll=senders <= GROUP)
+        gather_into(block_of, (within >= 0) & (index == begin + within) & (index < end))
+        amounts = jnp.where(lane == sender, end - begin, amounts)
+
+        first_r, last_r = bound(1, 0, after), bound(1, 1, after)
+        first_l, last_l = bound(2, 0, ahead), bound(0, 1, ahead)
+        middle = halo_before + (last_r - first_r)
+        chosen_r = (index >= first_r) & (index < last_r) & (index - first_r + halo_before == place)
+        chosen_l = (index >= first_l) & (index < last_l) & (index - first_l + middle == place)
+        gather_into(halo_block, chosen_r | chosen_l)
+        return middle + (last_l - first_l), amounts
+
+    halo_count, amounts = lax.fori_loop(
+        0,
+        senders,
+        per_sender,
+        (jnp.zeros((1, 1), I32), jnp.zeros((1, LANES), I32)),
+        unroll=senders <= GROUP,
+    )
 
     number = iota((stencil, LANES), 0).astype(F32)
     nowhere = float((height // LANES) * wide)
-    for i in range(slots // LANES):
-        line = line_sum[i]
+    for i in range(slots // LANES + 1):
+        line = line_sum[i, 0:stencil, :]
         leader = jnp.zeros(line.shape, F32)
         for k in reversed(range(stencil)):
             leader = jnp.where(line == line[k : k + 1, :], float(k), leader)
@@ -311,9 +339,17 @@
             here = (slot >= begin) & (slot < begin + BLOCK)
             found = jnp.max(jnp.where(here, batches, 0.0), axis=1, keepdims=True)
             most = jnp.where(here, found, most)
-        own_lines[top + stencil : top + stencil + 8, :] = jnp.where(
-            iota((8, LANES), 0) == 0, batches, most
-        ).astype(I32)
+        own_lines[top + stencil : top + stencil + 8, :] = jnp.concatenate(
+            [
+                batches.astype(I32),
+                most.astype(I32),
+                line_sum[i, stencil : stencil + 1, :].astype(I32),
+                amounts,
+                jnp.broadcast_to(halo_count, (1, LANES)),
+                jnp.zeros((3, LANES), I32),
+            ],
+            axis=0,
+        )
         codes = jnp.concatenate(
             [
                 jnp.zeros((CODES, LANES), F32),
@@ -481,11 +517,6 @@
         for copy in chunk_copies(chunk):
             copy.wait()
 
-    pending = []
-    if chunks == 1:
-        pending = chunk_copies(0)
-        for copy in pending:
-            copy.start()
     operands = [
         pltpu.make_async_copy(source, target, in_sems.at[i])
         for i, (source, target) in enumerate(
@@ -527,12 +558,11 @@
     zero_all([sums])
 
     lane_of = iota((slots, LANES), 1)
-    known = own[...]
+    room = slots + LANES
     column = 2 * stencil if first else 2 * stencil + 2
-    scale[...] = jnp.broadcast_to(known[:, column : column + 1], (slots, LANES))
+    scale[...] = jnp.broadcast_to(own[:, column : column + 1], (room, LANES))
+    known = own[0:slots, :]
     own_copy.wait()
-    if pending:
-        pending.pop(2).wait()
     if not first:
         merged_copy.wait()
 
@@ -552,10 +582,16 @@
         at = lax.shift_right_logical(slot, 7) * ((stencil + 7) * LANES) + slot
         return lines_s[at + k * LANES]
 
+    def amount_of(sender):
+        return lines_s[(stencil + 3) * LANES + sender]
+
+    halo_count = lines_s[(stencil + 4) * LANES]
+    halo_fits = halo_count <= LANES
+
     def batches_of(one, two):
         return jnp.maximum(own_line(one, stencil), own_line(two, stencil))
 
-    def own_groups(action):
+    def own_groups(action, halo):
         def group_at(top):
             top = pl.multiple_of(top, 8)
             most = own_line(top, stencil + 1)
@@ -568,26 +604,24 @@
             def _():
                 action(top, stencil)
 
-        if capacity % BLOCK or chunks > 1:
-
-            def step(i, carry):
-                group_at(i * BLOCK)
+        def blocks_of(top, amount):
+            def step(i, inner):
+                group_at(top + i * BLOCK)
+                return inner
+
+            lax.fori_loop(0, lax.div(amount + (BLOCK - 1), BLOCK), step, 0)
+
+        if capacity % BLOCK:
+            blocks_of(0, slots)
+        else:
+
+            def per_sender(sender, carry):
+                blocks_of(sender * capacity, amount_of(sender))
                 return carry
 
-            lax.fori_loop(0, slots // BLOCK, step, 0)
-        else:
-
-            def per_sender(sender, carry):
-                amount = start_of(sender, me, 0, 1) - start_of(sender, me, 0, 0)
-
-                def step(i, inner):
-                    group_at(sender * capacity + i * BLOCK)
-                    return inner
-
-                lax.fori_loop(0, lax.div(amount + (BLOCK - 1), BLOCK), step, 0)
-                return carry
-
             lax.fori_loop(0, senders, per_sender, 0)
+        if halo:
+            blocks_of(slots, jnp.minimum(halo_count, LANES))
 
     lane_f = iota((BLOCK, LANES), 1).astype(F32)
 
@@ -607,44 +641,45 @@
                 at = lane_f + float(LANES * place)
                 for k in range(place, stencil):
                     row = row + jnp.where(at == codes[k], weights[k], 0.0)
-            merged[pl.ds(place * slots + top, BLOCK), :] = row
+            merged[pl.ds(place * room + top, BLOCK), :] = row
 
     if first:
-        own_groups(build)
+        own_groups(build, True)
         merged_copy.start()
 
-    def own_pairs(chunk, action):
+    def own_pairs(action):
         def per_sender(sender, carry):
-            amount = start_of(sender, me, 0, 1) - start_of(sender, me, 0, 0)
-            base = (chunk * group + sender) * capacity
-            pairs(base, base + amount, action)
+            base = sender * capacity
+            pairs(base, base + amount_of(sender), action)
             return carry
 
-        lax.fori_loop(0, group, per_sender, 0)
-
-    def scatter_own(chunk):
-        def action(one, two, has_two):
-            second = jnp.where(has_two, 1.0, 0.0)
-            values = (scale[pl.ds(one, 1), :], scale[pl.ds(two, 1), :] * second)
-
-            def batch(begin):
-                todo = []
-                for slot, value, ref in zip((one, two), values, copies):
-                    for j in range(BATCH):
-                        line = own_line(slot, begin + j)
-                        row = merged[pl.ds((begin + j) * slots + slot, 1), :] * value
-                        todo.append((ref, line, ref[pl.ds(line, 1), :] + row))
-                for ref, line, row in todo:
-                    ref[pl.ds(line, 1), :] = row
-
-            def more(i, carry):
-                batch(i * BATCH)
-                return carry
-
-            batch(0)
-            lax.fori_loop(1, batches_of(one, two), more, 0)
-
-        own_pairs(chunk, action)
+        lax.fori_loop(0, senders, per_sender, 0)
+
+    def scatter_pair(one, two, values):
+        def batch(begin):
+            todo = []
+            for slot, value, ref in zip((one, two), values, copies):
+                for j in range(BATCH):
+                    line = own_line(slot, begin + j)
+                    row = merged[pl.ds((begin + j) * room + slot, 1), :] * value
+                    todo.append((ref, line, ref[pl.ds(line, 1), :] + row))
+            for ref, line, row in todo:
+                ref[pl.ds(line, 1), :] = row
+
+        def more(i, carry):
+            batch(i * BATCH)
+            return carry
+
+        batch(0)
+        lax.fori_loop(1, batches_of(one, two), more, 0)
+
+    def scatter_known(one, two, has_two):
+        second = jnp.where(has_two, 1.0, 0.0)
+        scatter_pair(one, two, (scale[pl.ds(one, 1), :], scale[pl.ds(two, 1), :] * second))
+
+    def scatter_sent(one, two, has_two):
+        second = jnp.where(has_two, val[own_line(two, stencil + 2)], 0.0)
+        scatter_pair(one, two, (val[own_line(one, stencil + 2)], second))
 
     def scatter_halo(chunk):
         def per_sender(sender, carry):
@@ -670,27 +705,23 @@
 
         lax.fori_loop(0, group, per_sender, 0)
 
-    def scatter_chunk(chunk):
-        scatter_own(chunk)
-        for copy in pending:
-            copy.wait()
-        scatter_halo(chunk)
-
-    def over_chunks(work):
-        if chunks == 1:
-            work(0)
-        else:
-
-            def step(chunk, carry):
-                load_chunk(chunk)
-                work(chunk)
-                return carry
-
-            lax.fori_loop(0, chunks, step, 0)
-
+    own_pairs(scatter_known)
     if not first:
         each_owner(lambda copy: copy.wait())
-    over_chunks(scatter_chunk)
+
+    @pl.when(halo_fits)
+    def _():
+        pairs(slots, slots + halo_count, scatter_known if first else scatter_sent)
+
+    @pl.when(jnp.logical_not(halo_fits))
+    def _():
+        def step(chunk, carry):
+            load_chunk(chunk)
+            scatter_halo(chunk)
+            return carry
+
+        lax.fori_loop(0, chunks, step, 0)
+
     for copy in operands:
         copy.wait()
 
@@ -740,41 +771,38 @@
         )
         outgoing[-1].start()
 
-    def gather_chunk(chunk):
-        def action(one, two, has_two):
-            def batch(begin, totals):
-                result = []
-                for slot, total in zip((one, two), totals):
-                    terms = []
-                    for j in range(BATCH):
-                        line = own_line(slot, begin + j)
-                        row = merged[pl.ds((begin + j) * slots + slot, 1), :]
-                        terms.append(row * smoothed[pl.ds(line, 1), :])
-                        if first:
-                            picked[pl.ds((begin + j) * slots + slot, 1), :] = std_flat[
-                                pl.ds(line, 1), :
-                            ]
-                    result.append(total + ((terms[0] + terms[1]) + (terms[2] + terms[3])))
-                return tuple(result)
-
-            zero = jnp.zeros((1, LANES), F32)
-            totals = lax.fori_loop(
-                1,
-                batches_of(one, two),
-                lambda i, totals: batch(i * BATCH, totals),
-                batch(0, (zero, zero)),
-            )
+    def gather_pair(one, two, has_two):
+        def batch(begin, totals):
+            result = []
             for slot, total in zip((one, two), totals):
-                sums[pl.ds(slot, 1), :] = total
-
-        own_pairs(chunk, action)
-
-    over_chunks(gather_chunk)
+                terms = []
+                for j in range(BATCH):
+                    line = own_line(slot, begin + j)
+                    row = merged[pl.ds((begin + j) * room + slot, 1), :]
+                    terms.append(row * smoothed[pl.ds(line, 1), :])
+                    if first:
+                        picked[pl.ds((begin + j) * room + slot, 1), :] = std_flat[
+                            pl.ds(line, 1), :
+                        ]
+                result.append(total + ((terms[0] + terms[1]) + (terms[2] + terms[3])))
+            return tuple(result)
+
+        zero = jnp.zeros((1, LANES), F32)
+        totals = lax.fori_loop(
+            1,
+            batches_of(one, two),
+            lambda i, totals: batch(i * BATCH, totals),
+            batch(0, (zero, zero)),
+        )
+        for slot, total in zip((one, two), totals):
+            sums[pl.ds(slot, 1), :] = total
+
+    own_pairs(gather_pair)
 
     def pick(top, places):
         info = own[pl.ds(top, BLOCK), :]
         codes = columns_of(info, CODES)
-        rows = [picked[pl.ds(place * slots + top, BLOCK), :] for place in range(places)]
+        rows = [picked[pl.ds(place * room + top, BLOCK), :] for place in range(places)]
         result = jnp.zeros((BLOCK, LANES), F32)
         for k in range(stencil):
             cell = jnp.zeros((BLOCK, LANES), F32)
@@ -786,14 +814,14 @@
         chosen[pl.ds(top, BLOCK), :] = result * info
 
     if first:
-        own_groups(pick)
+        own_groups(pick, False)
 
     def whole(x):
         return jnp.sum(x, axis=0, keepdims=True)
 
     total = jnp.sum(sums[...], axis=1, keepdims=True)
     lines = slots // LANES
-    known = own[...]
+    known = own[0:slots, :]
     source, weight, reply, image0 = (
         known[:, 2 * stencil + i : 2 * stencil + i + 1] for i in range(4)
     )
@@ -801,7 +829,8 @@
         reply = weight * total
         known = jnp.where(lane_of == 2 * stencil + 2, reply, known)
         known = jnp.where(lane_of == 2 * stencil + 3, total, known)
-        info_out[...] = known
+        info_out[0:slots, :] = known
+        info_out[slots:room, :] = own[slots:room, :]
         turned = known.T[2 * stencil + 2 : 2 * stencil + 3, :]
         message = [turned[:, i * LANES : (i + 1) * LANES] for i in range(lines)]
         message.append(
@@ -1070,6 +1099,7 @@
     capacity = 2 * hold // parts
     senders = parts
     slots = senders * capacity
+    room = slots + LANES
     rows_block = height // parts
     length = columns * parts
     blocks = height // LANES
@@ -1136,15 +1166,15 @@
         out_shape=[
             jax.ShapeDtypeStruct((layout.int_rows, LANES), I32),
             jax.ShapeDtypeStruct((layout.float_rows, LANES), F32),
-            jax.ShapeDtypeStruct((slots // LANES * (stencil + 8), LANES), I32),
-            jax.ShapeDtypeStruct((slots, LANES), F32),
+            jax.ShapeDtypeStruct((room // LANES * (stencil + 8), LANES), I32),
+            jax.ShapeDtypeStruct((room, LANES), F32),
         ],
         in_specs=[smem(), vmem()],
         out_specs=[vmem()] * 4,
         scratch_shapes=[
-            pltpu.VMEM((slots // LANES, LANES, LANES), F32),
-            pltpu.VMEM((slots // LANES, stencil, LANES), F32),
-            pltpu.VMEM((slots // LANES, stencil, LANES), F32),
+            pltpu.VMEM((room // LANES, LANES, LANES), F32),
+            pltpu.VMEM((room // LANES, stencil + 8, LANES), F32),
+            pltpu.VMEM((room // LANES, stencil, LANES), F32),
         ],
         compiler_params=params(),
         cost_estimate=cost(100),
@@ -1173,10 +1203,14 @@
         pltpu.SMEM((per,), I32),
         pltpu.SMEM((per,), F32),
         pltpu.SMEM((group * layout.table,), I32),
-        pltpu.SMEM((slots * (stencil + 8),), I32),
+        pltpu.SMEM((room * (stencil + 8),), I32),
     ]
     work = (
-        [column_slots, pltpu.VMEM((stencil * slots, LANES), F32), column_slots]
+        [
+            pltpu.VMEM((room, LANES), F32),
+            pltpu.VMEM((stencil * room, LANES), F32),
+            column_slots,
+        ]
         + [pltpu.VMEM((wide, height), BF)] * 2
         + [
             pltpu.VMEM((columns, height), F32),
@@ -1201,8 +1235,8 @@
         out_shape=[
             field_shape,
             jax.ShapeDtypeStruct((parts, reply_rows, LANES), F32),
-            jax.ShapeDtypeStruct((slots, LANES), F32),
-            jax.ShapeDtypeStruct((stencil * slots, LANES), F32),
+            jax.ShapeDtypeStruct((room, LANES), F32),
+            jax.ShapeDtypeStruct((stencil * room, LANES), F32),
         ],
         in_specs=[smem()] + [hbm()] * 3 + [vmem()] + [hbm()] * 5,
         out_specs=[hbm()] + [vmem()] * 2 + [hbm()],
@@ -1210,7 +1244,7 @@
         + [
             pltpu.SMEM((line,), F32),
             acc,
-            pltpu.VMEM((stencil * slots, LANES), F32),
+            pltpu.VMEM((stencil * room, LANES), F32),
             column_slots,
         ]
         + work,

time: 164 us -> 150 us (0.915)
  blocking collectives: 50.7 us -> 41.7 us
  Pallas kernels: 94.9 us -> 91.8 us
    all_to_all x1, blocking collectives: 28.3 us -> 23.3 us  [body(): lax.all_to_all(message, 'pencil', split_axis=0, concat_axis=0, tiled=True)]
    all_to_all x1, blocking collectives: 22.3 us -> 18.3 us  [body(): lax.all_to_all(sums, ('pencil', 'lev'), split_axis=0, concat_axis=0, tile...]
    pallas_call x1, Pallas kernels: 24.8 us -> 22.4 us  [body(): pl.pallas_call(functools.partial(apply_kernel, first=False, **static), ou...]
    pallas_call x1, Pallas kernels: 30.3 us -> 28.4 us  [body(): pl.pallas_call(functools.partial(apply_kernel, first=True, **static), out...]
  transfers between devices with their start and end apart: 3 -> 3, of which waited for: 1 -> 1; matrix products, arithmetic and copies ran while one was open for 1% -> 1% of each run, Pallas kernels for 6% -> 7%
where the time goes in v3:
time: 150 us
  Pallas kernels  91.8 us (61%)
  blocking collectives  41.7 us (28%)
  starting transfers between devices  12.1 us (8%)
  local copies, waits for them, and re-layouts  2.58 us (2%)
  between operations  1.51 us (1%)
    pallas_call x1, Pallas kernels, body(): pl.pallas_call(functools.partial(final_kernel, layout=layout, hold=hold,...  28.4 us
    pallas_call x1, Pallas kernels, body(): pl.pallas_call(functools.partial(apply_kernel, first=True, **static), out...  28.4 us
    all_to_all x1, blocking collectives, body(): lax.all_to_all(message, 'pencil', split_axis=0, concat_axis=0, tiled=True)  23.3 us
    pallas_call x1, Pallas kernels, body(): pl.pallas_call(functools.partial(apply_kernel, first=False, **static), ou...  22.4 us
    all_to_all x1, blocking collectives, body(): lax.all_to_all(sums, ('pencil', 'lev'), split_axis=0, concat_axis=0, tile...  18.3 us
    all_to_all x1, starting transfers between devices, body(): lax.all_to_all(packed, 'pencil', split_axis=0, concat_axis=0, tiled=True)  7.28 us
    pallas_call x1, Pallas kernels, body(): pl.pallas_call(functools.partial(bands_kernel, rows_block=row_size), out_...  6.26 us
    ppermute x1, starting transfers between devices, body(): std_r = lax.ppermute(std[:HALO, :], 'pencil', left)  4.77 us
  transfers between devices with their start and end apart: 3, of which 1 were waited for; matrix products, arithmetic and copies ran while one was open for 1% of the time, Pallas kernels for 7%

profile of v3, /device:TPU:0, one launch (start us, length us, event | category | flops | bytes accessed | tf_op | source)
XLA Modules:
  0.0 150.3 jit_solution(5952693798364347220)
XLA Ops:
  1.3 2.3 %pack.1 = f32[8,40,256]{2,1,0:T(8,128)} custom-call(s32[1]{0:T(128)S(6)} %copy.11.counts, s32[1,256]{1,0:T(1,128)} %bitcast.36, s32[16,256]{1,0:T(8,128)} %bitcast.34, f32[16,256]{1,0:T(8,128)} %bitcast.35, f32[1,256]{1,0:T(1,128)} %bitcast.37, f32[1,256]{1,0:T(1,128)} %bitcast.38), custom_call_target="tpu_custom_call" | custom-call | bytes 44280000 | tf_op jit(solution)/shard_map/pack/pallas_call | solution.py:1112
  3.6 7.3 %all-to-all-start = ((f32[8,40,256]{2,1,0:T(8,128)}), f32[8,40,256]{2,1,0:T(8,128)S(1)}, u32[]{:S(2)}, u32[]{:S(2)}) async-start(f32[8,40,256]{2,1,0:T(8,128)} %pack.1), calls=%async_computation | async-start | bytes 655360 | tf_op jit(solution)/shard_map/all_to_all | solution.py:1130
  10.9 1.1 slice_bitcast_fusion
  12.0 4.8 %collective-permute-start.1 = (f32[32,2048]{1,0:T(8,128)S(1)}, f32[32,2048]{1,0:T(8,128)S(1)}, u32[]{:S(2)}, u32[]{:S(2)}) collective-permute-start(f32[32,2048]{1,0:T(8,128)S(1)} %get-tuple-element.34), channel_id=1, source_target_pairs={{0,28},{4,0},{8,4},{12,8},{16,12},{20,16},{24,20},{28,24},{1,29},{... | collective-permute-start | bytes 786440 | tf_op jit(solution)/shard_map/ppermute | solution.py:1135
  16.7 0.0 collective-permute-start
  16.8 6.3 %bands.1 = (bf16[2,3,512,256]{3,2,1,0:T(8,128)(2,1)}, bf16[2,192,256]{2,1,0:T(8,128)(2,1)}, bf16[2,128,160]{2,1,0:T(8,128)(2,1)}, bf16[2,512,256]{2,1,0:T(8,128)(2,1)}) custom-call(f32[31]{0:T(128)} %bitcast.41, f32[31]{0:T(128)} %bitcast.42), custom_call_target="tpu_custom_call" | custom-call | bytes 22140000 | tf_op jit(solution)/shard_map/bands/pallas_call | solution.py:1139
  23.0 0.0 all-to-all-done.recv
  23.0 0.0 copy-start
  23.0 0.7 copy-done
  23.7 4.1 %unpack.1 = (s32[592,128]{1,0:T(8,128)}, f32[272,128]{1,0:T(8,128)}, s32[120,128]{1,0:T(8,128)}, f32[640,128]{1,0:T(8,128)}) custom-call(s32[1]{0:T(128)} %bitcast.meta.refs_0_, f32[8,40,256]{2,1,0:T(8,128)} %copy-done), custom_call_target="tpu_custom_call" | custom-call | bytes 369000 | tf_op jit(solution)/shard_map/unpack/pallas_call | solution.py:1155
  27.8 0.7 collective-permute-done.1.refs_7_.refs_9_
  28.5 0.0 copy-start.1
  28.5 0.0 collective-permute-done.refs_6_.refs_8_
  28.5 0.0 copy-start.2
  28.5 0.7 copy-done.1
  29.2 0.1 copy-done.2
  29.3 28.4 %apply_first.1 = (f32[512,2048]{1,0:T(8,128)}, f32[8,72,128]{2,1,0:T(8,128)}, f32[640,128]{1,0:T(8,128)}, f32[10240,128]{1,0:T(8,128)}) custom-call(s32[1]{0:T(128)} %bitcast.meta.refs_0_, s32[75776]{0:T(1024)} %bitcast.25, f32[34816]{0:T(1024)} %bitcast.28, s32[15360]{0:T(1024)} %bitcast.32, f32[640,128]{1,0:T(8,128)} %get-tuple-element.21.refs_4_, ...), custom_call_target="tpu_custom_call" | custom-call | tf_op jit(solution)/shard_map/apply_first/pallas_call | solution.py:1233
  57.7 23.3 %all_to_all.15.refs_6_ = f32[8,72,128]{2,1,0:T(8,128)} all-to-all(f32[8,72,128]{2,1,0:T(8,128)} %get-tuple-element.24), channel_id=1, replica_groups=mesh['pencil'=8,'lev'=4] {'pencil'}, dimensions={0} | all-to-all | bytes 589824 | tf_op jit(solution)/shard_map/all_to_all | solution.py:1255
  81.0 22.4 %apply_second.1 = (f32[512,2048]{1,0:T(8,128)}, f32[32,8,128]{2,1,0:T(8,128)}) custom-call(s32[1]{0:T(128)} %bitcast.meta.refs_0_, s32[75776]{0:T(1024)} %bitcast.26, f32[34816]{0:T(1024)} %bitcast.29, s32[15360]{0:T(1024)} %bitcast.33, f32[640,128]{1,0:T(8,128)} %get-tuple-element.25.refs_4_, f32[73728]{0:T(1024)} %bitcast.23, ...), custom_call_target="tpu_custom_call" | custom-call | tf_op jit(solution)/shard_map/apply_second/pallas_call | solution.py:1258
  103.4 18.3 %all_to_all.16 = f32[32,8,128]{2,1,0:T(8,128)} all-to-all(f32[32,8,128]{2,1,0:T(8,128)} %get-tuple-element.27), channel_id=1, replica_groups=mesh['pencil'=8,'lev'=4] {'pencil','lev'}, dimensions={0} | all-to-all | bytes 262144 | tf_op jit(solution)/shard_map/all_to_all | solution.py:1285
  121.7 28.4 %outputs.1 = (f32[256,4096]{1,0:T(8,128)}, f32[512,2048]{1,0:T(8,128)}) custom-call(s32[75776]{0:T(1024)} %bitcast.27, f32[34816]{0:T(1024)} %bitcast.30, f32[73728]{0:T(1024)} %bitcast.24, f32[8,4,8,128]{3,2,1,0:T(8,128)} %bitcast.31, f32[512,2048]{1,0:T(8,128)} %bitcast.22, f32[512,2048]{1,0:T(8,128)} %get-tuple-element.28.field0_h, ...), custom_call_target="tpu_custom_call" | custom-call | tf_op jit(solution)/shard_map/outputs/pallas_call | solution.py:1297
Async XLA Ops:
  3.6 19.4 %all-to-all-start = ((f32[8,40,256]{2,1,0:T(8,128)}), f32[8,40,256]{2,1,0:T(8,128)S(1)}, u32[]{:S(2)}, u32[]{:S(2)}) async-start(f32[8,40,256]{2,1,0:T(8,128)} %pack.1), calls=%async_computation | async-start | bytes 655360 | tf_op jit(solution)/shard_map/all_to_all | solution.py:1130
  12.0 16.5 %collective-permute-start.1 = (f32[32,2048]{1,0:T(8,128)S(1)}, f32[32,2048]{1,0:T(8,128)S(1)}, u32[]{:S(2)}, u32[]{:S(2)}) collective-permute-start(f32[32,2048]{1,0:T(8,128)S(1)} %get-tuple-element.34), channel_id=1, source_target_pairs={{0,28},{4,0},{8,4},{12,8},{16,12},{20,16},{24,20},{28,24},{1,29},{... | collective-permute-start | bytes 786440 | tf_op jit(solution)/shard_map/ppermute | solution.py:1135
  16.7 11.7 %collective-permute-start = (f32[32,2048]{1,0:T(8,128)S(1)}, f32[32,2048]{1,0:T(8,128)S(1)}, u32[]{:S(2)}, u32[]{:S(2)}) collective-permute-start(f32[32,2048]{1,0:T(8,128)S(1)} %get-tuple-element.35), channel_id=1, source_target_pairs={{0,4},{4,8},{8,12},{12,16},{16,20},{20,24},{24,28},{28,0},{1,5},{5... | collective-permute-start | bytes 786440 | tf_op jit(solution)/shard_map/ppermute | solution.py:1134
  23.0 0.7 copy-start
  28.5 0.7 copy-start.1
  28.5 0.8 copy-start.2

commit v4 on v3

--- a/solution.py
+++ b/solution.py
@@ -18,11 +18,12 @@
 PAD = 16
 PACK = 40
 GROUP = 8
-COPIES = 4
 PAIR = 2
 BATCH = 4
 BLOCK = 32
 CODES = 40
+STACK = 64
+LISTED = 512
 VMEM_LIMIT = 58 * 1024 * 1024
 
 
@@ -72,7 +73,7 @@
 
 
 def pack_kernel(
-    counts, owner, cells, weights, depart, prec, out, *, parts, columns, height, margin
+    counts, owner, cells, weights, depart, prec, out, marks, *, parts, columns, height, margin
 ):
     stencil, hold = cells.shape
     shift = height.bit_length() - 1
@@ -126,21 +127,25 @@
         tail = jnp.where(line == 5 + i, begins, tail)
     last = (line == 7) & (iota((8, hold), 1) == hold - 1)
 
-    def per_part(part, carry):
+    def mark(part, carry):
         low = part * block - margin
         high = (part + 1) * block + margin
         flag = jnp.where(live, any_of((row >= low) & (row < high)), 0.0)
-        place = jnp.sum(jnp.where(col_id < row_id, flag, 0.0), axis=1, keepdims=True)
-        chosen = (place == col_f) & (turn(flag) > 0.0)
-        listed = jnp.sum(jnp.where(chosen, rank_col, 0.0), axis=0, keepdims=True)
-        amount = jnp.sum(flag, axis=1, keepdims=True)
+        place = jnp.sum(jnp.where(row_id < col_id, turn(flag), 0.0), axis=0, keepdims=True)
+        marks[pl.ds(part, 1), :] = flag * (place + 1.0)
+        return carry
+
+    lax.fori_loop(0, parts, mark, 0, unroll=parts <= GROUP)
+    listed = marks[...]
+    amounts = jnp.max(listed, axis=1, keepdims=True)
+    listed = mm(listed.astype(BF), perm)
+    for part in range(parts):
         out[part, 0 : 2 * stencil, :] = ordered[0 : 2 * stencil, :]
         out[part, 2 * stencil : 2 * stencil + 8, :] = jnp.where(
-            line == 4, listed, jnp.where(last, amount, tail)
+            line == 4,
+            listed[part : part + 1, :],
+            jnp.where(last, amounts[part : part + 1, :], tail),
         )
-        return carry
-
-    lax.fori_loop(0, parts, per_part, 0, unroll=parts <= GROUP)
 
 
 class Layout:
@@ -164,33 +169,113 @@
         self.float_rows = at
 
 
+def right(x, by):
+    return lax.shift_right_logical(x, jnp.full(x.shape, by, I32))
+
+
+def nt(a, b):
+    return lax.dot_general(a, b, (((1,), (1,)), ((), ())), preferred_element_type=F32)
+
+
+class Received:
+    def __init__(self, recv, sender, me, *, parts, columns, height, capacity, stencil):
+        senders, _, hold = recv.shape
+        wide = columns + 2 * HALO
+        block = height // parts
+        high_rows = block + 2 * PAD
+        cell = recv[sender, 0:stencil, :].astype(I32)
+        self.tail = recv[sender, 2 * stencil : 2 * stencil + 8, :]
+        self.whole = self.tail.astype(I32)
+        self.pos = self.whole[3:4, :]
+        owner = right(self.whole[2:3, :], 2)
+        offset = owner - me
+        offset = jnp.where(offset > parts // 2, offset - parts, offset)
+        offset = jnp.where(offset < -(parts // 2), offset + parts, offset)
+        column = right(cell, height.bit_length() - 1)
+        row = cell & (height - 1)
+        at = offset * columns + column + HALO
+        self.addr = jnp.where(
+            (at >= 0) & (at < wide),
+            (right(row, 7) * wide + at) * LANES + (row & (LANES - 1)),
+            (height // LANES) * wide * LANES,
+        )
+        at_row = row - (block * me - PAD)
+        across = owner * columns + column
+        self.rows = jnp.where(
+            (at_row >= 0) & (at_row < high_rows) & (owner < parts),
+            (right(across, 7) * high_rows + at_row) * LANES + (across & (LANES - 1)),
+            (columns * parts // LANES) * high_rows * LANES,
+        )
+        self.owner = jnp.minimum(owner, parts - 1)
+        self.back = self.owner * (senders * capacity) + sender * capacity + self.pos
+
+
+def stack_of(addr, weights, tail, back):
+    hold = addr.shape[1]
+    rows = [
+        (addr & (LANES - 1)).astype(F32),
+        weights,
+        tail,
+        right(addr, 7).astype(F32),
+        back.astype(F32),
+        jnp.zeros((7, hold), F32),
+    ]
+    return jnp.concatenate(split3(jnp.concatenate(rows, axis=0)), axis=1)
+
+
+def gathered(stack, chosen):
+    select = jnp.where(chosen, 1.0, 0.0).astype(BF)
+    return nt(stack, jnp.concatenate([select] * 3, axis=1))
+
+
+def merge_lines(block, nowhere, stencil, extra):
+    number = iota((stencil, LANES), 0).astype(F32)
+    line = block[CODES : CODES + stencil, :]
+    leader = jnp.zeros(line.shape, F32)
+    for k in reversed(range(stencil)):
+        leader = jnp.where(line == line[k : k + 1, :], float(k), leader)
+    leads = jnp.where(leader == number, 1.0, 0.0)
+    count = jnp.zeros((1, LANES), F32)
+    ranks = []
+    for k in range(stencil):
+        ranks.append(count)
+        count = count + leads[k : k + 1, :]
+    place = jnp.zeros(line.shape, F32)
+    for k in range(stencil):
+        place = jnp.where(leader == float(k), ranks[k], place)
+    lists = []
+    for k in range(stencil):
+        found = jnp.where((leads > 0.0) & (place == float(k)), line, 0.0)
+        found = jnp.sum(found, axis=0, keepdims=True)
+        lists.append(jnp.where(count > float(k), found, nowhere))
+    batches = right(count.astype(I32) + (BATCH - 1), BATCH.bit_length() - 1)
+    most = jnp.zeros((1, LANES), F32)
+    slot = iota((1, LANES), 1)
+    for begin in range(0, LANES, BLOCK):
+        here = (slot >= begin) & (slot < begin + BLOCK)
+        found = jnp.max(jnp.where(here, batches.astype(F32), 0.0), axis=1, keepdims=True)
+        most = jnp.where(here, found, most)
+    back = block[CODES + stencil : CODES + stencil + 1, :]
+    ints = [jnp.concatenate(lists, axis=0).astype(I32), batches]
+    ints += [most.astype(I32), back.astype(I32)] + extra
+    ints = jnp.concatenate(ints, axis=0)
+    ints = jnp.concatenate([ints, jnp.zeros((stencil + 8 - ints.shape[0], LANES), I32)], axis=0)
+    rows = [
+        block[0:CODES, :],
+        place * float(LANES) + block[0:stencil, :],
+        jnp.zeros((LANES - CODES - stencil, LANES), F32),
+    ]
+    return ints, jnp.concatenate(rows, axis=0).T
+
+
 def unpack_kernel(
-    meta,
-    recv,
-    ints,
-    floats,
-    own_lines,
-    own,
-    own_sum,
-    line_sum,
-    lane_sum,
-    *,
-    layout,
-    parts,
-    columns,
-    height,
-    capacity,
-    stencil,
-    group,
+    meta, recv, ints, floats, own_lines, own, total, *, layout, group, **sizes
 ):
     senders, _, hold = recv.shape
     lines = hold // LANES
     me = meta[0]
-    shift = height.bit_length() - 1
-    wide = columns + 2 * HALO
-    block = height // parts
-    high_rows = block + 2 * PAD
-    length = columns * parts
+    parts, stencil, capacity = sizes["parts"], sizes["stencil"], sizes["capacity"]
+    wide = sizes["columns"] + 2 * HALO
     slots = senders * capacity
 
     def put(ref, place, sender, value):
@@ -205,15 +290,7 @@
                 for j in range(count):
                     ref[pl.ds(begin + sender * size + i + j * lines, 1), :] = part[j : j + 1]
 
-    def right(x, by):
-        return lax.shift_right_logical(x, jnp.full(x.shape, by, I32))
-
-    def nt(a, b):
-        return lax.dot_general(a, b, (((1,), (1,)), ((), ())), preferred_element_type=F32)
-
-    own_sum[...] = jnp.zeros(own_sum.shape, F32)
-    line_sum[...] = jnp.zeros(line_sum.shape, F32)
-    lane_sum[...] = jnp.zeros(lane_sum.shape, F32)
+    total[...] = jnp.zeros(total.shape, F32)
     place = iota((LANES, hold), 0)
     index = iota((LANES, hold), 1)
     lane = iota((1, LANES), 1)
@@ -223,70 +300,31 @@
 
     def per_sender(sender, carry):
         halo_before, amounts = carry
-        cell = recv[sender, 0:stencil, :].astype(I32)
-        tail = recv[sender, 2 * stencil : 2 * stencil + 8, :]
-        whole = tail.astype(I32)
-        key = whole[2:3, :]
-        pos = whole[3:4, :]
-        owner = right(key, 2)
-        offset = owner - me
-        offset = jnp.where(offset > parts // 2, offset - parts, offset)
-        offset = jnp.where(offset < -(parts // 2), offset + parts, offset)
-        column = right(cell, shift)
-        row = cell & (height - 1)
-        at = offset * columns + column + HALO
-        addr = jnp.where(
-            (at >= 0) & (at < wide),
-            (right(row, 7) * wide + at) * LANES + (row & (LANES - 1)),
-            (height // LANES) * wide * LANES,
-        )
-        at_row = row - (block * me - PAD)
-        across = owner * columns + column
-        rows = jnp.where(
-            (at_row >= 0) & (at_row < high_rows) & (owner < parts),
-            (right(across, 7) * high_rows + at_row) * LANES + (across & (LANES - 1)),
-            (length // LANES) * high_rows * LANES,
-        )
-        within = lax.rem(sender, group) * capacity + pos
-        owner = jnp.minimum(owner, parts - 1)
-        put(ints, layout.ints["addr"], sender, addr)
-        put(ints, layout.ints["rows"], sender, rows)
-        put(ints, layout.ints["listed"], sender, whole[4:5, :])
-        put(ints, layout.ints["slot"], sender, owner * (group * capacity) + within)
-        put(ints, layout.ints["start"], sender, whole[5:8, :])
-        put(floats, layout.floats["wgt"], sender, recv[sender, stencil : 2 * stencil, :])
-        put(floats, layout.floats["val"], sender, tail[0:1, :])
+        got = Received(recv, sender, me, **sizes)
+        weights = recv[sender, stencil : 2 * stencil, :]
+        within = lax.rem(sender, group) * capacity + got.pos
+        put(ints, layout.ints["addr"], sender, got.addr)
+        put(ints, layout.ints["rows"], sender, got.rows)
+        put(ints, layout.ints["listed"], sender, got.whole[4:5, :])
+        put(ints, layout.ints["slot"], sender, got.owner * (group * capacity) + within)
+        put(ints, layout.ints["start"], sender, got.whole[5:8, :])
+        put(floats, layout.floats["wgt"], sender, weights)
+        put(floats, layout.floats["val"], sender, got.tail[0:1, :])
 
         def bound(line, half, owner):
-            part = whole[5 + line : 6 + line, half * LANES : (half + 1) * LANES]
+            part = got.whole[5 + line : 6 + line, half * LANES : (half + 1) * LANES]
             return jnp.sum(jnp.where(lane == owner, part, 0), axis=1, keepdims=True)
 
-        at_lane = (addr & (LANES - 1)).astype(F32)
-        fields = jnp.concatenate([at_lane, recv[sender, stencil : 2 * stencil + 8, :]], axis=0)
-        fields = split3(fields)
-        back = owner * slots + sender * capacity + pos
-        lines_of = jnp.concatenate([right(addr, 7), back, jnp.zeros((7, hold), I32)], axis=0)
-        lines_of = split3(lines_of.astype(F32))
-
-        def gather_into(block_of, chosen):
-            select = jnp.where(chosen, 1.0, 0.0).astype(BF)
-            total = None
-            for part in fields:
-                term = nt(select, part)
-                total = term if total is None else total + term
-            own_sum[block_of, :, 0:CODES] += total
-            lane_sum[block_of] += nt(at_lane.astype(BF), select)
-            total = None
-            for part in lines_of:
-                term = nt(part, select)
-                total = term if total is None else total + term
-            line_sum[block_of] += total
+        stack = stack_of(got.addr, weights, got.tail, got.back)
 
         begin, end = bound(0, 0, me), bound(0, 1, me)
         first_slot = sender * capacity
         block_of = first_slot // LANES
         within = place - (first_slot - block_of * LANES)
-        gather_into(block_of, (within >= 0) & (index == begin + within) & (index < end))
+        chosen = (within >= 0) & (index == begin + within) & (index < end)
+        shift = first_slot - block_of * LANES
+        here = (lane >= shift) & (lane < shift + (end - begin))
+        total[block_of] = jnp.where(here, gathered(stack, chosen), total[block_of])
         amounts = jnp.where(lane == sender, end - begin, amounts)
 
         first_r, last_r = bound(1, 0, after), bound(1, 1, after)
@@ -294,8 +332,11 @@
         middle = halo_before + (last_r - first_r)
         chosen_r = (index >= first_r) & (index < last_r) & (index - first_r + halo_before == place)
         chosen_l = (index >= first_l) & (index < last_l) & (index - first_l + middle == place)
-        gather_into(halo_block, chosen_r | chosen_l)
-        return middle + (last_l - first_l), amounts
+        halo_after = middle + (last_l - first_l)
+        here = (lane >= halo_before) & (lane < halo_after)
+        values = gathered(stack, chosen_r | chosen_l)
+        total[halo_block] = jnp.where(here, values, total[halo_block])
+        return halo_after, amounts
 
     halo_count, amounts = lax.fori_loop(
         0,
@@ -304,61 +345,155 @@
         (jnp.zeros((1, 1), I32), jnp.zeros((1, LANES), I32)),
         unroll=senders <= GROUP,
     )
-
-    number = iota((stencil, LANES), 0).astype(F32)
-    nowhere = float((height // LANES) * wide)
+    extra = [amounts, jnp.broadcast_to(halo_count, (1, LANES))]
+    nowhere = float((sizes["height"] // LANES) * wide)
     for i in range(slots // LANES + 1):
-        line = line_sum[i, 0:stencil, :]
-        leader = jnp.zeros(line.shape, F32)
-        for k in reversed(range(stencil)):
-            leader = jnp.where(line == line[k : k + 1, :], float(k), leader)
-        leads = jnp.where(leader == number, 1.0, 0.0)
-        count = jnp.zeros((1, LANES), F32)
-        ranks = []
-        for k in range(stencil):
-            ranks.append(count)
-            count = count + leads[k : k + 1, :]
-        place = jnp.zeros(line.shape, F32)
-        for k in range(stencil):
-            place = jnp.where(leader == float(k), ranks[k], place)
-        lists = []
-        for k in range(stencil):
-            found = jnp.where((leads > 0.0) & (place == float(k)), line, 0.0)
-            found = jnp.sum(found, axis=0, keepdims=True)
-            lists.append(jnp.where(count > float(k), found, nowhere))
-        batches = lax.shift_right_logical(
-            count.astype(I32) + (BATCH - 1), jnp.full(count.shape, BATCH.bit_length() - 1, I32)
+        top = i * (stencil + 8)
+        own_lines[top : top + stencil + 8, :], own[i * LANES : (i + 1) * LANES, :] = merge_lines(
+            total[i], nowhere, stencil, extra
         )
-        lists = jnp.concatenate(lists, axis=0).astype(I32)
+
+
+def list_kernel(meta, recv, _, row_lines, row_data, total, **sizes):
+    senders, _, hold = recv.shape
+    stencil = sizes["stencil"]
+    high_rows = sizes["height"] // sizes["parts"] + 2 * PAD
+    place = iota((LISTED, hold), 0)
+    total[...] = jnp.zeros(total.shape, F32)
+
+    def per_sender(sender, before):
+        got = Received(recv, sender, meta[0], **sizes)
+        marks = got.whole[4:5, :]
+        zeros = jnp.zeros((stencil, hold), F32)
+        tail = jnp.concatenate([got.tail[0:1, :], zeros[0:7, :]], axis=0)
+        stack = stack_of(got.rows, zeros, tail, got.back)
+        values = gathered(stack, (marks > 0) & (marks - 1 + before == place))
+        after = before + got.whole[7:8, hold - 1 : hold]
+        slot = iota((1, LISTED), 1)
+        total[...] = jnp.where((slot >= before) & (slot < after), values, total[...])
+        return after
+
+    count = lax.fori_loop(
+        0, senders, per_sender, jnp.zeros((1, 1), I32), unroll=senders <= GROUP
+    )
+    nowhere = float((sizes["columns"] * sizes["parts"] // LANES) * high_rows)
+    for i in range(LISTED // LANES):
         top = i * (stencil + 8)
-        own_lines[top : top + stencil, :] = lists
-        batches = batches.astype(F32)
-        most = jnp.zeros((1, LANES), F32)
-        slot = iota((1, LANES), 1)
-        for begin in range(0, LANES, BLOCK):
-            here = (slot >= begin) & (slot < begin + BLOCK)
-            found = jnp.max(jnp.where(here, batches, 0.0), axis=1, keepdims=True)
-            most = jnp.where(here, found, most)
-        own_lines[top + stencil : top + stencil + 8, :] = jnp.concatenate(
-            [
-                batches.astype(I32),
-                most.astype(I32),
-                line_sum[i, stencil : stencil + 1, :].astype(I32),
-                amounts,
-                jnp.broadcast_to(halo_count, (1, LANES)),
-                jnp.zeros((3, LANES), I32),
-            ],
-            axis=0,
-        )
-        codes = jnp.concatenate(
-            [
-                jnp.zeros((CODES, LANES), F32),
-                place * float(LANES) + lane_sum[i],
-                jnp.zeros((LANES - CODES - stencil, LANES), F32),
-            ],
-            axis=0,
-        )
-        own[i * LANES : (i + 1) * LANES, :] = own_sum[i] + codes.T
+        block = total[:, i * LANES : (i + 1) * LANES]
+        (
+            row_lines[top : top + stencil + 8, :],
+            row_data[i * LANES : (i + 1) * LANES, :],
+        ) = merge_lines(block, nowhere, stencil, [jnp.broadcast_to(count, (1, LANES))])
+
+
+def word_of(table, slot, k, stencil):
+    at = lax.shift_right_logical(slot, 7) * ((stencil + 7) * LANES) + slot
+    return table[at + k * LANES]
+
+
+def columns_of(info, begin, stencil):
+    return [jnp.broadcast_to(info[:, begin + k : begin + k + 1], info.shape) for k in range(stencil)]
+
+
+def weight_rows(info, places, stencil):
+    lane_f = iota(info.shape, 1).astype(F32)
+    codes = columns_of(info, CODES, stencil)
+    weights = columns_of(info, stencil, stencil)
+    rows = []
+    for place in range(stencil):
+        row = jnp.zeros(info.shape, F32)
+        if place < places:
+            at = lane_f + float(LANES * place)
+            for k in range(place, stencil):
+                row = row + jnp.where(at == codes[k], weights[k], 0.0)
+        rows.append(row)
+    return rows
+
+
+def block_at(table, top, stencil, action):
+    top = pl.multiple_of(top, 8)
+    most = word_of(table, top, stencil + 1, stencil)
+
+    @pl.when(most <= 2)
+    def _():
+        action(top, 2 * BATCH)
+
+    @pl.when(most > 2)
+    def _():
+        action(top, stencil)
+
+
+def blocks_of(table, top, amount, stencil, action):
+    def step(i, carry):
+        block_at(table, top + i * BLOCK, stencil, action)
+        return carry
+
+    lax.fori_loop(0, lax.div(amount + (BLOCK - 1), BLOCK), step, 0)
+
+
+def factor_kernel(
+    lines_h, data, replies, _, merged_h, mixed, lines_s, table, merged, sems, *, stencil, slots
+):
+    parts = replies.shape[0]
+    lines = slots // LANES
+    lines_copy = pltpu.make_async_copy(lines_h, lines_s, sems.at[0])
+    lines_copy.start()
+
+    def per_owner(owner, carry):
+        for i in range(lines):
+            rows = [
+                jnp.zeros((stencil, LANES), F32),
+                replies[owner, pl.ds(8 + i, stencil, stride=lines), :],
+                jnp.zeros((1, LANES), F32),
+                replies[owner, i : i + 1, :],
+                jnp.zeros((LANES - 2 * stencil - 2, LANES), F32),
+            ]
+            at = pl.multiple_of(owner * slots + i * LANES, LANES)
+            table[pl.ds(at, LANES), :] = jnp.concatenate(rows, axis=0).T
+        return carry
+
+    lax.fori_loop(0, parts, per_owner, 0)
+    lines_copy.wait()
+    count = jnp.minimum(lines_s[(stencil + 3) * LANES], LISTED)
+
+    def mix(one, two, has_two):
+        for slot in (one, two):
+            back = word_of(lines_s, slot, stencil + 2, stencil)
+            mixed[pl.ds(slot, 1), :] = data[pl.ds(slot, 1), :] + table[pl.ds(back, 1), :]
+
+    pairs(0, count, mix)
+
+    def build(top, places):
+        rows = weight_rows(mixed[pl.ds(top, BLOCK), :], places, stencil)
+        for place, row in enumerate(rows):
+            merged[pl.ds(place * LISTED + top, BLOCK), :] = row
+
+    blocks_of(lines_s, 0, count, stencil, build)
+    merged_copy = pltpu.make_async_copy(merged, merged_h, sems.at[1])
+    merged_copy.start()
+    merged_copy.wait()
+
+
+def scatter_pair(table, merged, room, copies, one, two, values, stencil):
+    def batch(begin):
+        todo = []
+        for slot, value, ref in zip((one, two), values, copies):
+            for j in range(BATCH):
+                line = word_of(table, slot, begin + j, stencil)
+                row = merged[pl.ds((begin + j) * room + slot, 1), :] * value
+                todo.append((ref, line, ref[pl.ds(line, 1), :] + row))
+        for ref, line, row in todo:
+            ref[pl.ds(line, 1), :] = row
+
+    def more(i, carry):
+        batch(i * BATCH)
+        return carry
+
+    batch(0)
+    most = jnp.maximum(
+        word_of(table, one, stencil, stencil), word_of(table, two, stencil, stencil)
+    )
+    lax.fori_loop(1, most, more, 0)
 
 
 def band(shape, taps, shift):
@@ -579,8 +714,7 @@
         ]
 
     def own_line(slot, k):
-        at = lax.shift_right_logical(slot, 7) * ((stencil + 7) * LANES) + slot
-        return lines_s[at + k * LANES]
+        return word_of(lines_s, slot, k, stencil)
 
     def amount_of(sender):
         return lines_s[(stencil + 3) * LANES + sender]
@@ -592,55 +726,21 @@
         return jnp.maximum(own_line(one, stencil), own_line(two, stencil))
 
     def own_groups(action, halo):
-        def group_at(top):
-            top = pl.multiple_of(top, 8)
-            most = own_line(top, stencil + 1)
-
-            @pl.when(most <= 2)
-            def _():
-                action(top, 2 * BATCH)
-
-            @pl.when(most > 2)
-            def _():
-                action(top, stencil)
-
-        def blocks_of(top, amount):
-            def step(i, inner):
-                group_at(top + i * BLOCK)
-                return inner
-
-            lax.fori_loop(0, lax.div(amount + (BLOCK - 1), BLOCK), step, 0)
-
         if capacity % BLOCK:
-            blocks_of(0, slots)
+            blocks_of(lines_s, 0, slots, stencil, action)
         else:
 
             def per_sender(sender, carry):
-                blocks_of(sender * capacity, amount_of(sender))
+                blocks_of(lines_s, sender * capacity, amount_of(sender), stencil, action)
                 return carry
 
             lax.fori_loop(0, senders, per_sender, 0)
         if halo:
-            blocks_of(slots, jnp.minimum(halo_count, LANES))
-
-    lane_f = iota((BLOCK, LANES), 1).astype(F32)
-
-    def columns_of(info, begin):
-        return [
-            jnp.broadcast_to(info[:, begin + k : begin + k + 1], (BLOCK, LANES))
-            for k in range(stencil)
-        ]
+            blocks_of(lines_s, slots, jnp.minimum(halo_count, LANES), stencil, action)
 
     def build(top, places):
-        info = own[pl.ds(top, BLOCK), :]
-        codes = columns_of(info, CODES)
-        weights = columns_of(info, stencil)
-        for place in range(stencil):
-            row = jnp.zeros((BLOCK, LANES), F32)
-            if place < places:
-                at = lane_f + float(LANES * place)
-                for k in range(place, stencil):
-                    row = row + jnp.where(at == codes[k], weights[k], 0.0)
+        rows = weight_rows(own[pl.ds(top, BLOCK), :], places, stencil)
+        for place, row in enumerate(rows):
             merged[pl.ds(place * room + top, BLOCK), :] = row
 
     if first:
@@ -655,31 +755,15 @@
 
         lax.fori_loop(0, senders, per_sender, 0)
 
-    def scatter_pair(one, two, values):
-        def batch(begin):
-            todo = []
-            for slot, value, ref in zip((one, two), values, copies):
-                for j in range(BATCH):
-                    line = own_line(slot, begin + j)
-                    row = merged[pl.ds((begin + j) * room + slot, 1), :] * value
-                    todo.append((ref, line, ref[pl.ds(line, 1), :] + row))
-            for ref, line, row in todo:
-                ref[pl.ds(line, 1), :] = row
-
-        def more(i, carry):
-            batch(i * BATCH)
-            return carry
-
-        batch(0)
-        lax.fori_loop(1, batches_of(one, two), more, 0)
-
     def scatter_known(one, two, has_two):
         second = jnp.where(has_two, 1.0, 0.0)
-        scatter_pair(one, two, (scale[pl.ds(one, 1), :], scale[pl.ds(two, 1), :] * second))
+        values = (scale[pl.ds(one, 1), :], scale[pl.ds(two, 1), :] * second)
+        scatter_pair(lines_s, merged, room, copies, one, two, values, stencil)
 
     def scatter_sent(one, two, has_two):
         second = jnp.where(has_two, val[own_line(two, stencil + 2)], 0.0)
-        scatter_pair(one, two, (val[own_line(one, stencil + 2)], second))
+        values = (val[own_line(one, stencil + 2)], second)
+        scatter_pair(lines_s, merged, room, copies, one, two, values, stencil)
 
     def scatter_halo(chunk):
         def per_sender(sender, carry):
@@ -801,7 +885,8 @@
 
     def pick(top, places):
         info = own[pl.ds(top, BLOCK), :]
-        codes = columns_of(info, CODES)
+        codes = columns_of(info, CODES, stencil)
+        lane_f = iota(info.shape, 1).astype(F32)
         rows = [picked[pl.ds(place * room + top, BLOCK), :] for place in range(places)]
         result = jnp.zeros((BLOCK, LANES), F32)
         for k in range(stencil):
@@ -883,6 +968,9 @@
     ints,
     floats,
     replies_h,
+    lines_h,
+    merged_h,
+    mixed,
     totals,
     std_h,
     field0_h,
@@ -893,7 +981,6 @@
     increment_h,
     addr,
     listed,
-    start,
     slot,
     val,
     factors,
@@ -903,6 +990,9 @@
     control,
     high_s,
     low_s,
+    lines_s,
+    merged,
+    scale,
     *rest,
     layout,
     hold,
@@ -912,8 +1002,8 @@
     parts,
     length,
 ):
-    copies = rest[:COPIES]
-    sems, in_sems, out_sems = rest[COPIES:]
+    copies = rest[:PAIR]
+    sems, in_sems, out_sems = rest[PAIR:]
     group = min(GROUP, senders)
     chunks = senders // group
     per = stencil * hold
@@ -928,7 +1018,6 @@
         todo = [
             (ints, addr, layout.ints["rows"]),
             (ints, listed, layout.ints["listed"]),
-            (ints, start, layout.ints["start"]),
             (ints, slot, layout.ints["slot"]),
             (floats, val, layout.floats["val"]),
         ]
@@ -944,11 +1033,12 @@
         )
         return result
 
-    pending = []
-    if chunks == 1:
-        pending = chunk_copies(0)
-        for copy in pending:
-            copy.start()
+    listing = [
+        pltpu.make_async_copy(lines_h, lines_s, in_sems.at[3]),
+        pltpu.make_async_copy(merged_h, merged, in_sems.at[4]),
+    ]
+    for copy in listing:
+        copy.start()
     operands = [
         pltpu.make_async_copy(source, target, in_sems.at[i])
         for i, (source, target) in enumerate(
@@ -988,36 +1078,49 @@
 
     zero_all(copies)
 
+    data = mixed[...]
+    column = 2 * stencil
+    scale[...] = first * data[:, column : column + 1] + second * jnp.broadcast_to(
+        data[:, column + 1 : column + 2], data.shape
+    )
+    for copy in listing:
+        copy.wait()
+    count = lines_s[(stencil + 3) * LANES]
+
+    def add(one, two, has_two):
+        rest = jnp.where(has_two, 1.0, 0.0)
+        values = (scale[pl.ds(one, 1), :], scale[pl.ds(two, 1), :] * rest)
+        scatter_pair(lines_s, merged, LISTED, copies, one, two, values, stencil)
+
     def scatter_chunk():
         def per_sender(sender, carry):
-            def entries_of(at, scale):
-                idx = listed[sender * hold + at]
-                place = slot[sender * hold + idx]
-                place = place + lax.div(place, stride) * (owner_words - stride)
-                base = spot(sender, idx, per, stencil)
-                z0 = val[sender * hold + idx] * scale
-                u = factors[place] * scale
-                value = first_line * z0 + second_line * u
-                return [
-                    (addr[base + k * LANES], factors[place + to_factors + k * stride] * value)
-                    for k in range(stencil)
-                ]
-
-            def action(one, two, has_two):
-                scale = jnp.where(has_two, 1.0, 0.0)
-                scatter_entries(copies, entries_of(one, 1.0) + entries_of(two, scale), lane)
-
-            pairs(0, start[sender * layout.table + layout.table - 1], action)
+            def step(idx, inner):
+                @pl.when(listed[sender * hold + idx] > 0)
+                def _():
+                    place = slot[sender * hold + idx]
+                    place = place + lax.div(place, stride) * (owner_words - stride)
+                    base = spot(sender, idx, per, stencil)
+                    z0 = val[sender * hold + idx]
+                    value = first_line * z0 + second_line * factors[place]
+                    entries = [
+                        (addr[base + k * LANES], factors[place + to_factors + k * stride] * value)
+                        for k in range(stencil)
+                    ]
+                    scatter_entries(copies, entries, lane)
+
+                return inner
+
+            lax.fori_loop(0, hold, step, 0)
             return carry
 
         lax.fori_loop(0, group, per_sender, 0)
 
-    if chunks == 1:
-        for copy in pending:
-            copy.wait()
-        scatter_chunk()
-    else:
-
+    @pl.when(count <= LISTED)
+    def _():
+        pairs(0, count, add)
+
+    @pl.when(count > LISTED)
+    def _():
         def step(chunk, carry):
             for copy in chunk_copies(chunk):
                 copy.start()
@@ -1116,6 +1219,7 @@
         out_shape=jax.ShapeDtypeStruct((parts, PACK, hold), F32),
         in_specs=[smem()] + [vmem()] * 5,
         out_specs=vmem(),
+        scratch_shapes=[pltpu.VMEM((parts, hold), F32)],
         compiler_params=params(),
         cost_estimate=cost(12000),
         name="pack",
@@ -1152,17 +1256,11 @@
     )(x_kernel[0], y_kernel[0])
 
     meta = jnp.reshape(me, (1,)).astype(I32)
+    place = dict(
+        parts=parts, columns=columns, height=height, capacity=capacity, stencil=stencil
+    )
     ints, floats, own_lines, own = pl.pallas_call(
-        functools.partial(
-            unpack_kernel,
-            layout=layout,
-            parts=parts,
-            columns=columns,
-            height=height,
-            capacity=capacity,
-            stencil=stencil,
-            group=group,
-        ),
+        functools.partial(unpack_kernel, layout=layout, group=group, **place),
         out_shape=[
             jax.ShapeDtypeStruct((layout.int_rows, LANES), I32),
             jax.ShapeDtypeStruct((layout.float_rows, LANES), F32),
@@ -1172,9 +1270,7 @@
         in_specs=[smem(), vmem()],
         out_specs=[vmem()] * 4,
         scratch_shapes=[
-            pltpu.VMEM((room // LANES, LANES, LANES), F32),
-            pltpu.VMEM((room // LANES, stencil + 8, LANES), F32),
-            pltpu.VMEM((room // LANES, stencil, LANES), F32),
+            pltpu.VMEM((room // LANES, STACK, LANES), F32),
         ],
         compiler_params=params(),
         cost_estimate=cost(100),
@@ -1254,6 +1350,21 @@
 
     replies = lax.all_to_all(message, "pencil", split_axis=0, concat_axis=0, tiled=True)
     back = replies.reshape(-1)
+    line_rows = LISTED // LANES * (stencil + 8)
+    row_lines, row_data = pl.pallas_call(
+        functools.partial(list_kernel, **place),
+        out_shape=[
+            jax.ShapeDtypeStruct((line_rows, LANES), I32),
+            jax.ShapeDtypeStruct((LISTED, LANES), F32),
+        ],
+        in_specs=[smem(), vmem(), hbm()],
+        out_specs=[vmem()] * 2,
+        scratch_shapes=[pltpu.VMEM((STACK, LISTED), F32)],
+        compiler_params=params(),
+        cost_estimate=cost(4000),
+        name="list_rows",
+    )(meta, recv, info)
+    row_lines = row_lines.reshape(-1)
 
     field1, sums = pl.pallas_call(
         functools.partial(apply_kernel, first=False, **static),
@@ -1285,6 +1396,25 @@
     totals = lax.all_to_all(sums, ("pencil", "lev"), split_axis=0, concat_axis=0, tiled=True)
     totals = totals.reshape(parts, levels, 8, LANES)
 
+    listed_rows, mixed = pl.pallas_call(
+        functools.partial(factor_kernel, stencil=stencil, slots=slots),
+        out_shape=[
+            jax.ShapeDtypeStruct((stencil * LISTED, LANES), F32),
+            jax.ShapeDtypeStruct((LISTED, LANES), F32),
+        ],
+        in_specs=[hbm(), vmem(), vmem(), hbm()],
+        out_specs=[hbm(), vmem()],
+        scratch_shapes=[
+            pltpu.SMEM((line_rows * LANES,), I32),
+            pltpu.VMEM((parts * slots, LANES), F32),
+            pltpu.VMEM((stencil * LISTED, LANES), F32),
+            pltpu.SemaphoreType.DMA((2,)),
+        ],
+        compiler_params=params(),
+        cost_estimate=cost(8000),
+        name="factor_rows",
+    )(row_lines, row_data, replies, sums)
+
     by_chunk = back
     if chunks > 1:
         by_chunk = jnp.concatenate(
@@ -1309,12 +1439,11 @@
             jax.ShapeDtypeStruct((rows_block, length), F32),
             field_shape,
         ],
-        in_specs=[hbm()] * 3 + [vmem()] + [hbm()] * 3 + [vmem()] * 2,
+        in_specs=[hbm()] * 5 + [vmem()] * 2 + [hbm()] * 3 + [vmem()] * 2,
         out_specs=[hbm()] * 2,
         scratch_shapes=[
             pltpu.SMEM((per,), I32),
             pltpu.SMEM((line,), I32),
-            pltpu.SMEM((group * layout.table,), I32),
             pltpu.SMEM((line,), I32),
             pltpu.SMEM((line,), F32),
             pltpu.SMEM((parts * owner_words,), F32),
@@ -1324,16 +1453,32 @@
             pltpu.VMEM((rows_block, length), F32),
             pltpu.VMEM((rows_block, length), BF),
             pltpu.VMEM((rows_block, length), BF),
+            pltpu.SMEM((line_rows * LANES,), I32),
+            pltpu.VMEM((stencil * LISTED, LANES), F32),
+            pltpu.VMEM((LISTED, LANES), F32),
         ]
-        + [acc_rows] * COPIES
+        + [acc_rows] * PAIR
         + [
-            pltpu.SemaphoreType.DMA((7,)),
-            pltpu.SemaphoreType.DMA((3,)),
+            pltpu.SemaphoreType.DMA((5,)),
+            pltpu.SemaphoreType.DMA((5,)),
             pltpu.SemaphoreType.DMA((1 + length // WIDE,)),
         ],
         compiler_params=params(),
         name="outputs",
-    )(ints, floats, by_chunk, totals, std, field0, field1, lat1, lon1)
+    )(
+        ints,
+        floats,
+        by_chunk,
+        row_lines,
+        listed_rows,
+        mixed,
+        totals,
+        std,
+        field0,
+        field1,
+        lat1,
+        lon1,
+    )
     return control[None], increment[None]
 
 

time: 150 us -> 144 us (0.960)
  blocking collectives: 41.7 us -> 24.4 us
  starting transfers between devices: 12.1 us -> 19.2 us
    all_to_all x1 -> x0, blocking collectives: 18.3 us -> none  [body(): lax.all_to_all(sums, ('pencil', 'lev'), split_axis=0, concat_axis=0, tile...]
    pallas_call x1, Pallas kernels: 28.4 us -> 15.2 us  [body(): pl.pallas_call(functools.partial(final_kernel, layout=layout, hold=hold,...]
    pallas_call x1 -> x3, Pallas kernels: 4.08 us -> 16.7 us  [the longest x1 9.3 us: body(): pl.pallas_call(functools.partial(factor_kernel, stencil=stencil, slots=sl...]
    all_to_all x0 -> x1, starting transfers between devices: none -> 7.1 us  [body(): lax.all_to_all(sums, ('pencil', 'lev'), split_axis=0, concat_axis=0, tile...]
    pallas_call x1, Pallas kernels: 28.4 us -> 30 us  [body(): pl.pallas_call(functools.partial(apply_kernel, first=True, **static), out...]
  transfers between devices with their start and end apart: 3 -> 4, of which waited for: 1 -> 1; matrix products, arithmetic and copies ran while one was open for 1% -> 1% of each run, Pallas kernels for 7% -> 16%
where the time goes in v4:
time: 144 us; the launch traced here: 143 us
  Pallas kernels  93.1 us (65%)
  blocking collectives  24.4 us (17%)
  starting transfers between devices  19.2 us (13%)
  local copies, waits for them, and re-layouts  3.26 us (2%)
  between operations  1.54 us (1%)
    pallas_call x1, Pallas kernels, body(): pl.pallas_call(functools.partial(apply_kernel, first=True, **static), out...  30 us
    all_to_all x1, blocking collectives, body(): lax.all_to_all(message, 'pencil', split_axis=0, concat_axis=0, tiled=True)  24.4 us
    pallas_call x1, Pallas kernels, body(): pl.pallas_call(functools.partial(apply_kernel, first=False, **static), ou...  22.9 us
    pallas_call x1, Pallas kernels, body(): pl.pallas_call(functools.partial(final_kernel, layout=layout, hold=hold,...  15.2 us
    pallas_call x1, Pallas kernels, body(): pl.pallas_call(functools.partial(factor_kernel, stencil=stencil, slots=sl...  9.3 us
    all_to_all x1, starting transfers between devices, body(): lax.all_to_all(packed, 'pencil', split_axis=0, concat_axis=0, tiled=True)  7.28 us
    all_to_all x1, starting transfers between devices, body(): lax.all_to_all(sums, ('pencil', 'lev'), split_axis=0, concat_axis=0, tile...  7.1 us
    pallas_call x1, Pallas kernels, body(): pl.pallas_call(functools.partial(bands_kernel, rows_block=row_size), out_...  6.24 us
  transfers between devices with their start and end apart: 4, of which 1 were waited for; matrix products, arithmetic and copies ran while one was open for 1% of the time, Pallas kernels for 16%

profile of v4, /device:TPU:0, one launch (start us, length us, event | category | flops | bytes accessed | tf_op | source)
XLA Modules:
  0.0 142.8 jit_solution(16963073911724943170)
XLA Ops:
  1.3 2.2 %pack.1 = f32[8,40,256]{2,1,0:T(8,128)} custom-call(s32[1]{0:T(128)S(6)} %copy.11.counts, s32[1,256]{1,0:T(1,128)} %bitcast.39, s32[16,256]{1,0:T(8,128)} %bitcast.37, f32[16,256]{1,0:T(8,128)} %bitcast.38, f32[1,256]{1,0:T(1,128)} %bitcast.40, f32[1,256]{1,0:T(1,128)} %bitcast.41), custom_call_target="tpu_custom_call" | custom-call | bytes 44280000 | tf_op jit(solution)/shard_map/pack/pallas_call | solution.py:1215
  3.4 7.3 %all-to-all-start = ((f32[8,40,256]{2,1,0:T(8,128)}), f32[8,40,256]{2,1,0:T(8,128)S(1)}, u32[]{:S(2)}, u32[]{:S(2)}) async-start(f32[8,40,256]{2,1,0:T(8,128)} %pack.1), calls=%async_computation | async-start | bytes 655360 | tf_op jit(solution)/shard_map/all_to_all | solution.py:1234
  10.7 1.1 slice_bitcast_fusion
  11.8 4.8 %collective-permute-start.1 = (f32[32,2048]{1,0:T(8,128)S(1)}, f32[32,2048]{1,0:T(8,128)S(1)}, u32[]{:S(2)}, u32[]{:S(2)}) collective-permute-start(f32[32,2048]{1,0:T(8,128)S(1)} %get-tuple-element.42), channel_id=1, source_target_pairs={{0,28},{4,0},{8,4},{12,8},{16,12},{20,16},{24,20},{28,24},{1,29},{... | collective-permute-start | bytes 786440 | tf_op jit(solution)/shard_map/ppermute | solution.py:1239
  16.6 0.0 collective-permute-start
  16.6 6.2 %bands.1 = (bf16[2,3,512,256]{3,2,1,0:T(8,128)(2,1)}, bf16[2,192,256]{2,1,0:T(8,128)(2,1)}, bf16[2,128,160]{2,1,0:T(8,128)(2,1)}, bf16[2,512,256]{2,1,0:T(8,128)(2,1)}) custom-call(f32[31]{0:T(128)} %bitcast.44, f32[31]{0:T(128)} %bitcast.45), custom_call_target="tpu_custom_call" | custom-call | bytes 22140000 | tf_op jit(solution)/shard_map/bands/pallas_call | solution.py:1243
  22.8 0.0 all-to-all-done.recv
  22.8 0.0 copy-start
  22.8 0.7 copy-done
  23.5 3.5 %unpack.1 = (s32[592,128]{1,0:T(8,128)}, f32[272,128]{1,0:T(8,128)}, s32[120,128]{1,0:T(8,128)}, f32[640,128]{1,0:T(8,128)}) custom-call(s32[1]{0:T(128)} %bitcast.meta.refs_0_, f32[8,40,256]{2,1,0:T(8,128)} %copy-done), custom_call_target="tpu_custom_call" | custom-call | bytes 369000 | tf_op jit(solution)/shard_map/unpack/pallas_call | solution.py:1262
  27.0 1.3 collective-permute-done.1.refs_7_.refs_9_
  28.3 0.0 copy-start.1
  28.3 0.0 collective-permute-done.refs_6_.refs_8_
  28.3 0.0 copy-start.2
  28.3 0.7 copy-done.1
  29.0 0.1 copy-done.2
  29.1 30.0 %apply_first.1 = (f32[512,2048]{1,0:T(8,128)}, f32[8,72,128]{2,1,0:T(8,128)}, f32[640,128]{1,0:T(8,128)}, f32[10240,128]{1,0:T(8,128)}) custom-call(s32[1]{0:T(128)} %bitcast.meta.refs_0_, s32[75776]{0:T(1024)} %bitcast.26, f32[34816]{0:T(1024)} %bitcast.29, s32[15360]{0:T(1024)} %bitcast.33, f32[640,128]{1,0:T(8,128)} %get-tuple-element.25.refs_4_, ...), custom_call_target="tpu_custom_call" | custom-call | tf_op jit(solution)/shard_map/apply_first/pallas_call | solution.py:1329
  59.1 24.4 %all_to_all.15.refs_6_.replies = f32[8,72,128]{2,1,0:T(8,128)} all-to-all(f32[8,72,128]{2,1,0:T(8,128)} %get-tuple-element.28), channel_id=1, replica_groups=mesh['pencil'=8,'lev'=4] {'pencil'}, dimensions={0} | all-to-all | bytes 589824 | tf_op jit(solution)/shard_map/all_to_all | solution.py:1351
  83.5 22.9 %apply_second.1 = (f32[512,2048]{1,0:T(8,128)}, f32[32,8,128]{2,1,0:T(8,128)}) custom-call(s32[1]{0:T(128)} %bitcast.meta.refs_0_, s32[75776]{0:T(1024)} %bitcast.27, f32[34816]{0:T(1024)} %bitcast.30, s32[15360]{0:T(1024)} %bitcast.34, f32[640,128]{1,0:T(8,128)} %get-tuple-element.29._.refs_4_, f32[73728]{0:T(1024)} %bitcast.24, ...), custom_call_target="tpu_custom_call" | custom-call | tf_op jit(solution)/shard_map/apply_second/pallas_call | solution.py:1369
  106.4 7.1 %all-to-all-start.2 = ((f32[32,8,128]{2,1,0:T(8,128)}), f32[32,8,128]{2,1,0:T(8,128)S(1)}, u32[]{:S(2)}, u32[]{:S(2)}) async-start(f32[32,8,128]{2,1,0:T(8,128)} %get-tuple-element.33._), calls=%async_computation.2 | async-start | bytes 262144 | tf_op jit(solution)/shard_map/all_to_all | solution.py:1396
  113.5 4.0 %list_rows.1 = (s32[96,128]{1,0:T(8,128)}, f32[512,128]{1,0:T(8,128)}) custom-call(s32[1]{0:T(128)} %bitcast.meta.refs_0_, f32[8,40,256]{2,1,0:T(8,128)} %copy-done, f32[640,128]{1,0:T(8,128)} %get-tuple-element.29._.refs_4_), custom_call_target="tpu_custom_call" | custom-call | bytes 14760000 | tf_op jit(solution)/shard_map/list_rows/pallas_call | solution.py:1354
  117.5 9.3 %factor_rows.1 = (f32[8192,128]{1,0:T(8,128)}, f32[512,128]{1,0:T(8,128)}) custom-call(s32[12288]{0:T(1024)} %bitcast.35, f32[512,128]{1,0:T(8,128)} %get-tuple-element.31.data, f32[8,72,128]{2,1,0:T(8,128)} %all_to_all.15.refs_6_.replies, f32[32,8,128]{2,1,0:T(8,128)} %get-tuple-element.33._), custom_call_target="tpu_custom_call" | custom-call | bytes 29520000 | tf_op jit(solution)/shard_map/factor_rows/pallas_call | solution.py:1399
  126.8 0.0 all-to-all-done.2
  126.8 0.0 copy-start.3
  126.8 0.6 copy-done.3
  127.5 15.2 %outputs.1 = (f32[256,4096]{1,0:T(8,128)}, f32[512,2048]{1,0:T(8,128)}) custom-call(s32[75776]{0:T(1024)} %bitcast.28, f32[34816]{0:T(1024)} %bitcast.31, f32[73728]{0:T(1024)} %bitcast.25, s32[12288]{0:T(1024)} %bitcast.36, f32[8192,128]{1,0:T(8,128)} %get-tuple-element.34.merged_h, f32[512,128]{1,0:T(8,128)} %get-tuple-element.35.mixed, ...), custom_call_target="tpu_custom_call" | custom-call | tf_op jit(solution)/shard_map/outputs/pallas_call | solution.py:1427
Async XLA Ops:
  3.4 19.4 %all-to-all-start = ((f32[8,40,256]{2,1,0:T(8,128)}), f32[8,40,256]{2,1,0:T(8,128)S(1)}, u32[]{:S(2)}, u32[]{:S(2)}) async-start(f32[8,40,256]{2,1,0:T(8,128)} %pack.1), calls=%async_computation | async-start | bytes 655360 | tf_op jit(solution)/shard_map/all_to_all | solution.py:1234
  11.8 16.5 %collective-permute-start.1 = (f32[32,2048]{1,0:T(8,128)S(1)}, f32[32,2048]{1,0:T(8,128)S(1)}, u32[]{:S(2)}, u32[]{:S(2)}) collective-permute-start(f32[32,2048]{1,0:T(8,128)S(1)} %get-tuple-element.42), channel_id=1, source_target_pairs={{0,28},{4,0},{8,4},{12,8},{16,12},{20,16},{24,20},{28,24},{1,29},{... | collective-permute-start | bytes 786440 | tf_op jit(solution)/shard_map/ppermute | solution.py:1239
  16.6 11.7 %collective-permute-start = (f32[32,2048]{1,0:T(8,128)S(1)}, f32[32,2048]{1,0:T(8,128)S(1)}, u32[]{:S(2)}, u32[]{:S(2)}) collective-permute-start(f32[32,2048]{1,0:T(8,128)S(1)} %get-tuple-element.43), channel_id=1, source_target_pairs={{0,4},{4,8},{8,12},{12,16},{16,20},{20,24},{24,28},{28,0},{1,5},{5... | collective-permute-start | bytes 786440 | tf_op jit(solution)/shard_map/ppermute | solution.py:1238
  22.8 0.7 copy-start
  28.3 0.7 copy-start.1
  28.3 0.8 copy-start.2
  106.4 20.4 %all-to-all-start.2 = ((f32[32,8,128]{2,1,0:T(8,128)}), f32[32,8,128]{2,1,0:T(8,128)S(1)}, u32[]{:S(2)}, u32[]{:S(2)}) async-start(f32[32,8,128]{2,1,0:T(8,128)} %get-tuple-element.33._), calls=%async_computation.2 | async-start | bytes 262144 | tf_op jit(solution)/shard_map/all_to_all | solution.py:1396
  126.8 0.7 copy-start.3
